TPU v7x, 512 devices: a whole 4x8x8 slice. The times are simulated.
512 devices in a mesh: row: 16 (over x, z_hi), col: 32 (over y, z_lo, core).
Axes of the slice: x: 4, y: 8, z: 8 (z_hi: 4, z_lo: 2; z = z_hi * 2 + z_lo), core: 2. Of those that a mesh axis runs over, the one named last changes fastest.
Arguments:
- features: bfloat16 [32768, 256], P(('col', 'row')), may hold values from -6 to 6
- cotangent: bfloat16 [32768, 256], P(('col', 'row')), may hold values from -0.09375 to 0.09375
- w_first: bfloat16 [256, 256], replicated, may hold values from -0.375 to 0.375
- w_second: bfloat16 [256, 256], replicated, may hold values from -0.375 to 0.375
- adjacency_tiles: bfloat16 [16, 32, 64, 128, 128], P('row', 'col'), may hold values from -0.046875 to 0.046875
- tile_ids: int32 [16, 32, 2, 64], P('row', 'col'), may hold values from 0 to 7, as said below
- counts: int32 [16, 32], P('row', 'col'), may hold values from 16 to 64, as said below
Outputs:
- item_out: bfloat16 [32768, 256], P(('col', 'row'))
- grad_w1: float32 [256, 256], replicated
- grad_w2: float32 [256, 256], replicated
Inputs may be any that keep to these rules, and one draw needn't show every extreme that they name: `tile_ids`: in every block each of the 64 tile positions occurs exactly once over the 64 slots. A block holds either 64 live slots or at most 32; blocks with 64 live slots have r < 8 and c < 16; only the first counts[r, c] slots of a block are live.
All inputs are finite; a program needn't handle non-finite values.
Results may differ from a plain program's by a relative error of at most 0.018.
Values may be sent and summed in bfloat16 or wider, within the bound.
No kernel may reach another device: no remote copies, remote signals or barrier semaphores. Data moves between devices by JAX's collectives and lax.ppermute only.
A program may use at most 64 MiB of HBM per device.

v0:
```python
import jax
import jax.numpy as jnp
from jax import lax
from jax.sharding import PartitionSpec as P

GROUP = 8
ROW_TILES = 8
COL_TILES = 8


def tile_product(slot_tiles, slot_ids, live_count, dense_block, transposed, out_blocks):
    tile_size = slot_tiles.shape[1]
    feat_width = dense_block.shape[1]
    source = dense_block.reshape(-1, tile_size, feat_width)
    turn_count = (live_count + GROUP - 1) // GROUP
    slot_index = jnp.arange(GROUP, dtype=jnp.int32)

    def advance(turn, running):
        first_slot = turn * GROUP
        group_tiles = lax.dynamic_slice_in_dim(slot_tiles, first_slot, GROUP, 0)
        group_ids = lax.dynamic_slice_in_dim(slot_ids, first_slot, GROUP, 1)
        live_mask = (first_slot + slot_index < live_count).astype(jnp.float32)
        if transposed:
            picked = source[group_ids[0]]
            products = jnp.einsum(
                "gji,gjf->gif", group_tiles, picked, preferred_element_type=jnp.float32
            )
            target = group_ids[1]
        else:
            picked = source[group_ids[1]]
            products = jnp.einsum(
                "gij,gjf->gif", group_tiles, picked, preferred_element_type=jnp.float32
            )
            target = group_ids[0]
        return running.at[target].add(products * live_mask[:, None, None])

    start = jnp.zeros((out_blocks, tile_size, feat_width), jnp.float32)
    running = lax.fori_loop(0, turn_count, advance, start)
    return running.reshape(out_blocks * tile_size, feat_width)


def shards(features, cotangent, w_first, w_second, adjacency_tiles, tile_ids, counts):
    slot_tiles = adjacency_tiles[0, 0]
    slot_ids = tile_ids[0, 0]
    own_count = counts[0, 0]

    def users_from_items(item_block):
        running = tile_product(slot_tiles, slot_ids, own_count, item_block, False, ROW_TILES)
        return running

    def items_from_users(user_block):
        running = tile_product(slot_tiles, slot_ids, own_count, user_block, True, COL_TILES)
        return running

    def user_sums(item_local):
        item_block = lax.all_gather(item_local, "row", axis=0, tiled=True)
        partial_sum = users_from_items(item_block)
        return lax.psum_scatter(partial_sum, "col", scatter_dimension=0, tiled=True)

    def item_sums(user_local):
        user_block = lax.all_gather(user_local, "col", axis=0, tiled=True)
        partial_sum = items_from_users(user_block)
        return lax.psum_scatter(
            partial_sum.astype(jnp.bfloat16), "row", scatter_dimension=0, tiled=True
        ).astype(jnp.float32)

    projected = jnp.dot(features, w_first, preferred_element_type=jnp.float32).astype(jnp.bfloat16)
    z_first = user_sums(projected)
    d_users = user_sums(cotangent).astype(jnp.bfloat16)
    gate_sig = jax.nn.sigmoid(z_first)
    hidden = (z_first * gate_sig).astype(jnp.bfloat16)
    mapped = jnp.dot(hidden, w_second, preferred_element_type=jnp.float32).astype(jnp.bfloat16)
    item_out = item_sums(mapped).astype(jnp.bfloat16)
    second_part = jnp.einsum("uf,ug->fg", hidden, d_users, preferred_element_type=jnp.float32)
    back = jnp.einsum("ug,fg->uf", d_users, w_second, preferred_element_type=jnp.float32)
    d_pre = (back * gate_sig * (1.0 + z_first * (1.0 - gate_sig))).astype(jnp.bfloat16)
    e_items = item_sums(d_pre).astype(jnp.bfloat16)
    first_part = jnp.einsum("if,ig->fg", features, e_items, preferred_element_type=jnp.float32)
    grad_w1, grad_w2 = lax.psum((first_part, second_part), ("row", "col"))
    return (item_out, grad_w1, grad_w2)


def solution(mesh):
    return jax.shard_map(
        shards,
        mesh=mesh,
        in_specs=(
            P(("col", "row"), None),
            P(("col", "row"), None),
            P(),
            P(),
            P("row", "col", None, None, None),
            P("row", "col", None, None),
            P("row", "col"),
        ),
        out_specs=(P(("col", "row"), None), P(), P()),
        check_vma=False,
    )
```

profile of v0, /device:TPU:1, one launch (start us, length us, event | category | flops | bytes accessed | tf_op | source)
XLA Modules:
  0.0 856.5 jit_solution(16690656661422684454)
XLA Ops:
  9.0 45.6 %all_gather.12 = bf16[1024,256]{1,0:T(8,128)(2,1)S(1)} all-gather(bf16[64,256]{1,0:T(8,128)(2,1)S(1)} %convolution_convert_fusion), channel_id=1, replica_groups=mesh['row'=16,'col'=32] {'row'}, dimensions={0}, use_global_device_ids=true | all-gather | bytes 557056 | tf_op jit(solution)/shard_map/all_gather | solution.py:56
  54.7 37.0 %while.44 = (s32[]{:T(128)}, f32[8,128,256]{2,1,0:T(8,128)S(1)}, s32[]{:T(128)}, s32[2,64]{1,0:T(2,128)}, bf16[64,128,128]{2,1,0:T(8,128)(2,1)}, /*index=5*/bf16...) while((s32[]{:T(128)}, f32[8,128,256]{2,1,0:T(8,128)S(1)}, ...), condition=%wide.region_2.3_spmd.clone, body=%wide.region_0.2_spmd.clone.sunk | while | flops 67634256 | bytes 6033995 | solution.py:38
  58.0 1.3 scatter_fusion
  76.5 1.3 scatter_fusion
  81.1 1.3 scatter_fusion
  85.8 1.3 scatter_fusion
  90.4 1.3 scatter_fusion
  92.8 35.6 %all_gather.14 = bf16[1024,256]{1,0:T(8,128)(2,1)S(1)} all-gather(bf16[64,256]{1,0:T(8,128)(2,1)S(1)} %copy-done.5), channel_id=1, replica_groups=mesh['row'=16,'col'=32] {'row'}, dimensions={0}, use_global_device_ids=true | all-gather | bytes 557056 | tf_op jit(solution)/shard_map/all_gather | solution.py:56
  128.5 31.6 %while.46 = (s32[]{:T(128)}, f32[8,128,256]{2,1,0:T(8,128)S(1)}, s32[]{:T(128)}, s32[2,64]{1,0:T(2,128)S(1)}, bf16[64,128,128]{2,1,0:T(8,128)(2,1)}, /*index=5*/...) while((s32[]{:T(128)}, f32[8,128,256]{2,1,0:T(8,128)S(1)}, ...), condition=%wide.region_10.11_spmd.clone, body=%wide.region_8.10_spmd.clone.sunk | while | flops 67634256 | bytes 6033995 | solution.py:38
  131.1 1.3 scatter_fusion.2
  150.9 1.3 scatter_fusion.2
  154.8 1.3 scatter_fusion.2
  158.8 1.3 scatter_fusion.2
  161.2 4.1 copy.10
  165.3 43.6 %reduce-scatter.5.cloned.1.call-done = f32[32,256]{1,0:T(8,128)} async-done(((f32[1024,256]{1,0:T(8,128)}), f32[32,256]{1,0:T(8,128)}) %reduce-scatter.5.cloned.1.call-update) | async-done | bytes 32784 | tf_op jit(solution)/shard_map/reduce_scatter | solution.py:58
  208.9 120.1 %reduce-scatter.9.cloned.1.call-done = f32[32,256]{1,0:T(8,128)} async-done(((f32[1024,256]{1,0:T(8,128)}), f32[32,256]{1,0:T(8,128)}) %reduce-scatter.9.cloned.1.call-update) | async-done | bytes 32784 | tf_op jit(solution)/shard_map/reduce_scatter | solution.py:58
  330.0 35.1 %all_gather.15 = bf16[1024,256]{1,0:T(8,128)(2,1)S(1)} all-gather(bf16[32,256]{1,0:T(8,128)(2,1)S(1)} %fusion.25), channel_id=1, replica_groups=mesh['row'=16,'col'=32] {'col'}, dimensions={0}, use_global_device_ids=true | all-gather | bytes 540672 | tf_op jit(solution)/shard_map/all_gather | solution.py:61
  365.2 31.6 %while.47 = (s32[]{:T(128)}, f32[8,128,256]{2,1,0:T(8,128)S(1)}, s32[]{:T(128)}, s32[2,64]{1,0:T(2,128)S(1)}, bf16[64,128,128]{1,2,0:T(8,128)(2,1)}, /*index=5*/...) while((s32[]{:T(128)}, f32[8,128,256]{2,1,0:T(8,128)S(1)}, ...), condition=%wide.region_14.15_spmd.clone, body=%wide.region_12.14_spmd.clone.sunk | while | flops 67634256 | bytes 6033995 | solution.py:38
  371.8 1.3 scatter_fusion.3
  387.6 1.3 scatter_fusion.3
  391.5 1.3 scatter_fusion.3
  398.9 32.2 %all_gather.13 = bf16[1024,256]{1,0:T(8,128)(2,1)S(1)} all-gather(bf16[32,256]{1,0:T(8,128)(2,1)S(1)} %convolution_convert_fusion.1), channel_id=1, replica_groups=mesh['row'=16,'col'=32] {'col'}, dimensions={0}, use_global_device_ids=true | all-gather | bytes 540672 | tf_op jit(solution)/shard_map/all_gather | solution.py:61
  431.0 51.2 %reduce-scatter.11.cloned.1.call-done = bf16[64,256]{1,0:T(8,128)(2,1)} async-done(((bf16[1024,256]{1,0:T(8,128)(2,1)}), bf16[64,256]{1,0:T(8,128)(2,1)}) %reduce-scatter.11.cloned.1.call-update) | async-done | bytes 32784 | tf_op jit(solution)/shard_map/reduce_scatter | solution.py:63
  482.3 1.7 convolution_bitcast_fusion
  484.1 31.6 %while.45 = (s32[]{:T(128)}, f32[8,128,256]{2,1,0:T(8,128)S(1)}, s32[]{:T(128)}, s32[2,64]{1,0:T(2,128)S(1)}, bf16[64,128,128]{1,2,0:T(8,128)(2,1)}, /*index=5*/...) while((s32[]{:T(128)}, f32[8,128,256]{2,1,0:T(8,128)S(1)}, ...), condition=%wide.region_6.7_spmd.clone, body=%wide.region_4.6_spmd.clone.sunk | while | flops 67634256 | bytes 6033995 | solution.py:38
  490.7 1.3 scatter_fusion.1
  506.5 1.3 scatter_fusion.1
  510.4 1.3 scatter_fusion.1
  516.6 241.3 %all-reduce.3.cloned.1.call-done = (f32[256,256]{0,1:T(8,128)}, f32[256,256]{1,0:T(8,128)}) async-done(((f32[256,256]{0,1:T(8,128)}, f32[256,256]{1,0:T(8,128)}), (f32[256,256]{0,1:T(8,128)}, f32[256,256]{1,0:T(8,128)})) %all-reduce.3.cloned.1.call-update) | async-done | bytes 524304 | tf_op jit(solution)/shard_map/psum | solution.py:79
  757.9 1.8 copy.13
  759.7 88.6 %reduce-scatter.7.cloned.1.call-done = bf16[64,256]{1,0:T(8,128)(2,1)} async-done(((bf16[1024,256]{1,0:T(8,128)(2,1)}), bf16[64,256]{1,0:T(8,128)(2,1)}) %reduce-scatter.7.cloned.1.call-update) | async-done | bytes 32784 | tf_op jit(solution)/shard_map/reduce_scatter | solution.py:63
  848.3 1.7 copy.47
  (247 shorter events, 117.5 us)
Async XLA Ops:
  7.2 0.9 copy-start
  7.2 201.7 %reduce-scatter.5.cloned.1.call-start = ((), (), s32[]{:S(2)}) async-start(), calls=%async_computation.4 | async-start | bytes 1081344 | tf_op jit(solution)/shard_map/reduce_scatter | solution.py:58
  54.7 38.1 %copy-start.5 = (bf16[64,256]{1,0:T(8,128)(2,1)S(1)}, bf16[64,256]{1,0:T(8,128)(2,1)}, u32[]{:S(2)}) copy-start(bf16[64,256]{1,0:T(8,128)(2,1)} %param.16) | copy-start | bytes 98308
  91.7 1.0 copy-start.1
  91.8 36.8 %copy-start.3 = (s32[2,64]{1,0:T(2,128)S(1)}, s32[2,64]{1,0:T(2,128)}, u32[]{:S(2)}) copy-start(s32[2,64]{1,0:T(2,128)} %get-tuple-element.679) | copy-start | bytes 1540
  92.8 236.3 %reduce-scatter.9.cloned.1.call-start = ((), (), s32[]{:S(2)}) async-start(), calls=%async_computation.6 | async-start | bytes 1081344 | tf_op jit(solution)/shard_map/reduce_scatter | solution.py:58
  160.2 1.0 copy-start.2
  161.2 167.9 %copy-start.8 = (bf16[256,256]{1,0:T(8,128)(2,1)S(1)}, bf16[256,256]{1,0:T(8,128)(2,1)}, u32[]{:S(2)}) copy-start(bf16[256,256]{1,0:T(8,128)(2,1)} %param.18) | copy-start | bytes 393220
  161.2 321.1 %reduce-scatter.11.cloned.1.call-start = ((), (), s32[]{:S(2)}) async-start(), calls=%async_computation.7 | async-start | bytes 557056 | tf_op jit(solution)/shard_map/reduce_scatter | solution.py:63
  396.8 1.0 copy-start.6
  396.8 1.1 copy-start.7
  396.8 85.5 %copy-start.4 = (bf16[64,256]{1,0:T(8,128)(2,1)S(1)}, bf16[64,256]{1,0:T(8,128)(2,1)}, u32[]{:S(2)}) copy-start(bf16[64,256]{1,0:T(8,128)(2,1)} %param.15) | copy-start | bytes 98308
  397.7 360.2 %all-reduce.3.cloned.1.call-start = ((), (), s32[]{:S(2)}) async-start(), calls=%async_computation.8 | async-start | bytes 1048576 | tf_op jit(solution)/shard_map/psum | solution.py:79
  484.0 364.4 %reduce-scatter.7.cloned.1.call-start = ((), (), s32[]{:S(2)}) async-start(), calls=%async_computation.5 | async-start | bytes 557056 | tf_op jit(solution)/shard_map/reduce_scatter | solution.py:63
Sparse Core Ops, SparseCore 0:
  92.9 116.0 reduce-scatter.4
  211.9 117.0 reduce-scatter.8
  397.8 84.4 reduce-scatter.10
  488.7 269.1 all-reduce.2
  762.4 85.9 reduce-scatter.6
where the time goes:
time: 860 us; the launch traced here: 857 us
  waiting for transfers between devices  545 us (63%)
  blocking collectives  149 us (17%)
  other arithmetic  65.5 us (8%)
  matrix products  44.5 us (5%)
  local copies, waits for them, and re-layouts  36.4 us (4%)
  between operations  14.6 us (2%)
    psum x1, waiting for transfers between devices, shards(): grad_w1, grad_w2 = lax.psum((first_part, second_part), ('row', 'col'))  241 us
    reduce_scatter x2, waiting for transfers between devices, user_sums(): return lax.psum_scatter(partial_sum, 'col', scatter_dimension=0, tiled=True)  164 us
    reduce_scatter x2, waiting for transfers between devices, item_sums(): lax.psum_scatter(partial_sum.astype(jnp.bfloat16), 'row', scatter_dimensi...  140 us
    all_gather x2, blocking collectives, user_sums(): item_block = lax.all_gather(item_local, 'row', axis=0, tiled=True)  81.3 us
    all_gather x2, blocking collectives, item_sums(): user_block = lax.all_gather(user_local, 'col', axis=0, tiled=True)  67.3 us
    scatter-add x32, other arithmetic, advance(): return running.at[target].add(products * live_mask[:, None, None])  42.5 us
    convert_element_type x32, other arithmetic, advance(): live_mask = (first_slot + slot_index < live_count).astype(jnp.float32)  20.8 us
    dot_general x16, matrix products, advance(): jnp.einsum('gji,gjf->gif', group_tiles, picked, preferred_element_type=jn...  20 us
  transfers between devices with their start and end apart: 5, of which 5 were waited for; matrix products, arithmetic and copies ran while one was open for 8% of the time, Pallas kernels for 0%

commit v1 on v0

v1 whole, which is shorter than its diff:
```python
import jax
import jax.numpy as jnp
from jax import lax
from jax.experimental import pallas as pl
from jax.experimental.pallas import tpu as pltpu
from jax.sharding import PartitionSpec as P

TILE = 128
N_ROW = 16
N_COL = 32
SLOTS = 64
BLOCK = 1024
WIDTH = 256
USERS = BLOCK // N_COL
ITEMS = BLOCK // N_ROW
GRADS = 2 * WIDTH // N_COL
VMEM = pl.BlockSpec(memory_space=pltpu.VMEM)
SMEM = pl.BlockSpec(memory_space=pltpu.SMEM)
f32 = jnp.float32
bf16 = jnp.bfloat16


def params():
    return pltpu.CompilerParams(vmem_limit_bytes=40 * 1024 * 1024)


def cost(flops, moved):
    return pl.CostEstimate(flops=flops, bytes_accessed=moved, transcendentals=0)


def dense_kernel(ids, count, tiles, dense, turned):
    def place(k, carry):
        r = pl.multiple_of(ids[0, k] * TILE, TILE)
        c = pl.multiple_of(ids[1, k] * TILE, TILE)
        tile = jnp.where(k < count[0, 0], tiles[k], jnp.zeros((TILE, TILE), bf16))
        dense[pl.ds(r, TILE), pl.ds(c, TILE)] = tile
        turned[pl.ds(c, TILE), pl.ds(r, TILE)] = tile.T
        return carry

    lax.fori_loop(0, SLOTS, place, 0)


def make_dense(ids, count, tiles):
    shape = jax.ShapeDtypeStruct((BLOCK, BLOCK), bf16)
    return pl.pallas_call(
        dense_kernel,
        out_shape=(shape, shape),
        in_specs=[SMEM, SMEM, VMEM],
        out_specs=(VMEM, VMEM),
        compiler_params=params(),
        cost_estimate=cost(0, 3 * 2 * BLOCK * BLOCK),
        name="dense_block",
    )(ids, count, tiles)


def middle_kernel(parts, w_first, w_second, out):
    total = parts[0].astype(f32)
    for i in range(1, N_COL):
        total = total + parts[i].astype(f32)
    sums = total[:, :WIDTH]
    d_users = total[:, WIDTH:].astype(bf16)
    high = sums.astype(bf16)
    low = (sums - high.astype(f32)).astype(bf16)
    w1 = w_first[...]
    w2 = w_second[...]
    z = jnp.dot(high, w1, preferred_element_type=f32) + jnp.dot(low, w1, preferred_element_type=f32)
    s = jax.nn.sigmoid(z)
    hidden = (z * s).astype(bf16)
    mapped = jnp.dot(hidden, w2, preferred_element_type=f32).astype(bf16)
    back = lax.dot_general(d_users, w2, (((1,), (1,)), ((), ())), preferred_element_type=f32)
    d_pre = (back * s * (1.0 + z * (1.0 - s))).astype(bf16)
    over_users = (((0,), (0,)), ((), ()))
    grad_one = lax.dot_general(high, d_pre, over_users, preferred_element_type=f32) + lax.dot_general(
        low, d_pre, over_users, preferred_element_type=f32
    )
    grad_two = lax.dot_general(hidden, d_users, over_users, preferred_element_type=f32)
    half = GRADS // 2
    for i in range(N_COL):
        out[i, :USERS] = mapped
        both = jnp.concatenate([grad_one[i * half : (i + 1) * half], grad_two[i * half : (i + 1) * half]], axis=0)
        out[i, USERS:] = both.astype(bf16)


def middle(parts, w_first, w_second):
    return pl.pallas_call(
        middle_kernel,
        out_shape=jax.ShapeDtypeStruct((N_COL, USERS + GRADS, WIDTH), bf16),
        in_specs=[VMEM, VMEM, VMEM],
        out_specs=VMEM,
        compiler_params=params(),
        name="middle",
    )(parts, w_first, w_second)


def back_kernel(got, turned, out, mapped):
    grads = got[0, USERS:].astype(f32)
    for i in range(1, N_COL):
        grads = grads + got[i, USERS:].astype(f32)
    for i in range(N_COL):
        mapped[i * USERS : (i + 1) * USERS] = got[i, :USERS]
    grads = grads.astype(bf16)
    for i in range(N_ROW):
        out[i, ITEMS:] = grads
    per = 4
    rows = per * ITEMS
    for i in range(N_ROW // per):
        part = jnp.dot(turned[i * rows : (i + 1) * rows], mapped[...], preferred_element_type=f32).astype(bf16)
        for j in range(per):
            out[i * per + j, :ITEMS] = part[j * ITEMS : (j + 1) * ITEMS]


def back_product(got, turned):
    return pl.pallas_call(
        back_kernel,
        out_shape=jax.ShapeDtypeStruct((N_ROW, ITEMS + GRADS, WIDTH), bf16),
        in_specs=[VMEM, VMEM],
        out_specs=VMEM,
        scratch_shapes=[pltpu.VMEM((BLOCK, WIDTH), bf16)],
        compiler_params=params(),
        name="back_product",
    )(got, turned)


def shards(features, cotangent, w_first, w_second, adjacency_tiles, tile_ids, counts):
    both = jnp.concatenate([features, cotangent], axis=1)
    spread = jnp.broadcast_to(both[None], (N_ROW, ITEMS, 2 * WIDTH))
    dense, turned = make_dense(tile_ids[0, 0], counts, adjacency_tiles[0, 0])
    items = lax.all_to_all(spread, "row", 0, 0).reshape(BLOCK, 2 * WIDTH)
    partial = jnp.dot(dense, items, preferred_element_type=f32).astype(bf16)
    parts = lax.all_to_all(partial.reshape(N_COL, USERS, 2 * WIDTH), "col", 0, 0)
    sent = middle(parts, w_first, w_second)
    got = lax.all_to_all(sent, "col", 0, 0)
    sent = back_product(got, turned)
    got = lax.all_to_all(sent, "row", 0, 0)
    grads = jnp.sum(got[:, ITEMS:].astype(f32), axis=0).astype(bf16)
    item_out = jnp.sum(got[:, :ITEMS].astype(f32), axis=0).astype(bf16)
    grads = lax.all_to_all(jnp.broadcast_to(grads[None], (N_COL, GRADS, WIDTH)), "col", 0, 0)
    half = GRADS // 2
    grad_one = grads[:, :half].astype(f32).reshape(WIDTH, WIDTH)
    grad_two = grads[:, half:].astype(f32).reshape(WIDTH, WIDTH)
    return (item_out, grad_one, grad_two)


def solution(mesh):
    return jax.shard_map(
        shards,
        mesh=mesh,
        in_specs=(
            P(("col", "row"), None),
            P(("col", "row"), None),
            P(),
            P(),
            P("row", "col", None, None, None),
            P("row", "col", None, None),
            P("row", "col"),
        ),
        out_specs=(P(("col", "row"), None), P(), P()),
        check_vma=False,
    )
```

time: 860 us -> 156 us (0.18)
  waiting for transfers between devices: 545 us -> 24.7 us
  other arithmetic: 65.5 us -> 2.32 us
  blocking collectives: 149 us -> 91.3 us
  matrix products: 44.5 us -> 2.86 us
  local copies, waits for them, and re-layouts: 36.4 us -> 4.75 us
  starting transfers between devices: 0.2 us -> 21.7 us
  between operations: 14.6 us -> 1.38 us
    reduce_scatter x4 -> x0, waiting for transfers between devices: 304 us -> none  [the longest x2 164 us: user_sums(): return lax.psum_scatter(partial_sum, 'col', scatter_dimension=0, tiled=True)]
    psum x1 -> x0, waiting for transfers between devices: 241 us -> none  [shards(): grad_w1, grad_w2 = lax.psum((first_part, second_part), ('row', 'col'))]
    all_gather x4 -> x0, blocking collectives: 149 us -> none  [the longest x2 81.3 us: user_sums(): item_block = lax.all_gather(item_local, 'row', axis=0, tiled=True)]
    all_to_all x0 -> x3, blocking collectives: none -> 91.3 us  [the longest x1 44 us: shards(): lax.all_to_all(partial.reshape(N_COL, USERS, 2 * WIDTH), 'col', 0, 0)]
    scatter-add x32 -> x0, other arithmetic: 42.5 us -> none  [advance(): return running.at[target].add(products * live_mask[:, None, None])]
    dot_general x37 -> x1, matrix products: 44.5 us -> 2.86 us  [shards(): partial = jnp.dot(dense, items, preferred_element_type=f32).astype(bf16)]
    all_to_all x0 -> x2, waiting for transfers between devices: none -> 24.7 us  [the longest x1 13.9 us: shards(): items = lax.all_to_all(spread, 'row', 0, 0).reshape(BLOCK, 2 * WIDTH)]
    convert_element_type x34 -> x0, other arithmetic: 22.5 us -> none  [the longest x32 20.8 us: advance(): live_mask = (first_slot + slot_index < live_count).astype(jnp.float32)]
  transfers between devices with their start and end apart: 5 -> 2, of which waited for: 5 -> 2; matrix products, arithmetic and copies ran while one was open for 8% -> 0% of each run, Pallas kernels for 0% -> 4%
where the time goes in v1:
time: 156 us
  blocking collectives  91.3 us (59%)
  waiting for transfers between devices  24.7 us (16%)
  starting transfers between devices  21.7 us (14%)
  Pallas kernels  6.9 us (4%)
  local copies, waits for them, and re-layouts  4.75 us (3%)
  matrix products  2.86 us (2%)
  other arithmetic  2.32 us (1%)
    all_to_all x1, blocking collectives, shards(): lax.all_to_all(partial.reshape(N_COL, USERS, 2 * WIDTH), 'col', 0, 0)  44 us
    all_to_all x1, blocking collectives, shards(): got = lax.all_to_all(sent, 'col', 0, 0)  26.7 us
    all_to_all x1, blocking collectives, shards(): got = lax.all_to_all(sent, 'row', 0, 0)  20.7 us
    all_to_all x1, waiting for transfers between devices, shards(): items = lax.all_to_all(spread, 'row', 0, 0).reshape(BLOCK, 2 * WIDTH)  13.9 us
    all_to_all x1, starting transfers between devices, shards(): items = lax.all_to_all(spread, 'row', 0, 0).reshape(BLOCK, 2 * WIDTH)  13.4 us
    all_to_all x1, waiting for transfers between devices, shards(): lax.all_to_all(jnp.broadcast_to(grads[None], (N_COL, GRADS, WIDTH)), 'col...  10.7 us
    all_to_all x1, starting transfers between devices, shards(): lax.all_to_all(jnp.broadcast_to(grads[None], (N_COL, GRADS, WIDTH)), 'col...  8.32 us
    pallas_call x1, Pallas kernels, make_dense(): pl.pallas_call(dense_kernel, out_shape=(shape, shape), in_specs=[SMEM, SM...  5.5 us
  transfers between devices with their start and end apart: 2, of which 2 were waited for; matrix products, arithmetic and copies ran while one was open for 0% of the time, Pallas kernels for 4%

profile of v1, /device:TPU:1, one launch (start us, length us, event | category | flops | bytes accessed | tf_op | source)
XLA Modules:
  0.0 156.0 jit_solution(10680159127267817195)
XLA Ops:
  0.6 0.0 copy-start.3
  0.6 0.8 pad_maximum_fusion
  1.4 1.1 broadcast_in_dim.4
  2.5 13.4 %all-to-all-start = ((bf16[16,64,512]{2,1,0:T(8,128)(2,1)}), bf16[16,64,512]{2,1,0:T(8,128)(2,1)S(1)}, u32[]{:S(2)}, u32[]{:S(2)}) async-start(bf16[16,64,512]{2,1,0:T(8,128)(2,1)} %broadcast_in_dim.4), calls=%async_computation | async-start | bytes 2097152 | tf_op jit(solution)/shard_map/all_to_all | solution.py:128
  16.6 0.0 copy-done.3
  16.6 0.0 copy-start
  16.6 1.6 %copy-done = bf16[1,1,64,128,128]{4,3,2,1,0:T(8,128)(2,1)S(1)} copy-done((bf16[1,1,64,128,128]{4,3,2,1,0:T(8,128)(2,1)S(1)}, bf16[1,1,64,128,128]{4,3,2,1,0:T(8,128)(2,1)}, u32[]{:S(2)}) %copy-start) | copy-done | bytes 2097176
  18.2 5.5 %dense_block.1 = (bf16[1024,1024]{1,0:T(8,128)(2,1)S(1)}, bf16[1024,1024]{1,0:T(8,128)(2,1)S(1)}) custom-call(s32[2,64]{1,0:T(2,128)S(1)} %bitcast.17, s32[1,1]{1,0:T(1,128)S(6)} %copy.10.count, bf16[64,128,128]{2,1,0:T(8,128)(2,1)S(1)} %bitcast.16), custom_call_target="tpu_custom_call" | custom-call | bytes 6291456 | tf_op jit(solution)/shard_map/dense_block/pallas_call | solution.py:45
  23.7 0.0 copy-start.4
  23.7 1.3 copy-done.4
  25.0 13.9 %all-to-all-done = bf16[16,64,512]{2,1,0:T(8,128)(2,1)S(1)} async-done(((bf16[16,64,512]{2,1,0:T(8,128)(2,1)}), bf16[16,64,512]{2,1,0:T(8,128)(2,1)S(1)}, u32[]{:S(2)}, u32[]{:S(2)}) %all-to-all-start) | async-done | bytes 1048608 | tf_op jit(solution)/shard_map/all_to_all | solution.py:128
  39.0 2.9 %convolution_convert_fusion = bf16[1024,512]{1,0:T(8,128)(2,1)S(1)} fusion(bf16[1024,1024]{1,0:T(8,128)(2,1)} %copy-done.4, bf16[1024,512]{1,0:T(8,128)(2,1)S(1)} %bitcast.18), kind=kOutput, calls=%fused_computation | convolution fusion | flops 1074266112 | bytes 4194304 | tf_op jit(solution)/shard_map/dot_general | solution.py:129
  41.8 0.0 copy-start.1
  41.9 0.0 copy-start.2
  41.9 44.0 %all_to_all.25.parts = bf16[32,32,512]{2,1,0:T(8,128)(2,1)S(1)} all-to-all(bf16[32,32,512]{2,1,0:T(8,128)(2,1)S(1)} %bitcast.19), channel_id=1, replica_groups=mesh['row'=16,'col'=32] {'col'}, dimensions={0} | all-to-all | bytes 2097152 | tf_op jit(solution)/shard_map/all_to_all | solution.py:130
  85.8 0.0 copy-done.1
  85.8 0.0 copy-done.2
  85.8 0.7 middle.1
  86.5 26.7 %all_to_all.26.got = bf16[32,48,256]{2,1,0:T(8,128)(2,1)S(1)} all-to-all(bf16[32,48,256]{2,1,0:T(8,128)(2,1)S(1)} %middle.1), channel_id=1, replica_groups=mesh['row'=16,'col'=32] {'col'}, dimensions={0} | all-to-all | bytes 1572864 | tf_op jit(solution)/shard_map/all_to_all | solution.py:132
  113.2 0.7 back_product.1
  113.9 20.7 %all_to_all.27 = bf16[16,80,256]{2,1,0:T(8,128)(2,1)S(1)} all-to-all(bf16[16,80,256]{2,1,0:T(8,128)(2,1)S(1)} %back_product.1), channel_id=1, replica_groups=mesh['row'=16,'col'=32] {'row'}, dimensions={0} | all-to-all | bytes 1310720 | tf_op jit(solution)/shard_map/all_to_all | solution.py:134
  134.6 0.7 broadcast_in_dim.5
  135.4 8.3 %all-to-all-start.4 = ((bf16[32,16,256]{2,1,0:T(8,128)(2,1)}), bf16[32,16,256]{2,1,0:T(8,128)(2,1)S(1)}, u32[]{:S(2)}, u32[]{:S(2)}) async-start(bf16[32,16,256]{2,1,0:T(8,128)(2,1)} %broadcast_in_dim.5), calls=%async_computation.4 | async-start | bytes 524288 | tf_op jit(solution)/shard_map/all_to_all | solution.py:137
  143.7 0.7 slice_reduce_fusion
  144.4 10.7 %all-to-all-done.4 = bf16[32,16,256]{2,1,0:T(8,128)(2,1)S(1)} async-done(((bf16[32,16,256]{2,1,0:T(8,128)(2,1)}), bf16[32,16,256]{2,1,0:T(8,128)(2,1)S(1)}, u32[]{:S(2)}, u32[]{:S(2)}) %all-to-all-start.4) | async-done | bytes 262176 | tf_op jit(solution)/shard_map/all_to_all | solution.py:137
  155.1 0.8 fusion
  (1 shorter events, 0.0 us)
Async XLA Ops:
  0.6 16.0 %copy-start.3 = (s32[1,1,2,64]{3,2,1,0:T(2,128)S(1)}, s32[1,1,2,64]{3,2,1,0:T(2,128)}, u32[]{:S(2)}) copy-start(s32[1,1,2,64]{3,2,1,0:T(2,128)} %param.12) | copy-start | bytes 1540
  2.5 36.5 %all-to-all-start = ((bf16[16,64,512]{2,1,0:T(8,128)(2,1)}), bf16[16,64,512]{2,1,0:T(8,128)(2,1)S(1)}, u32[]{:S(2)}, u32[]{:S(2)}) async-start(bf16[16,64,512]{2,1,0:T(8,128)(2,1)} %broadcast_in_dim.4), calls=%async_computation | async-start | bytes 2097152 | tf_op jit(solution)/shard_map/all_to_all | solution.py:128
  16.6 1.6 %copy-start = (bf16[1,1,64,128,128]{4,3,2,1,0:T(8,128)(2,1)S(1)}, bf16[1,1,64,128,128]{4,3,2,1,0:T(8,128)(2,1)}, u32[]{:S(2)}) copy-start(bf16[1,1,64,128,128]{4,3,2,1,0:T(8,128)(2,1)} %param.11) | copy-start | bytes 6291460
  23.7 1.3 copy-start.4
  41.8 44.0 %copy-start.1 = (bf16[256,256]{1,0:T(8,128)(2,1)S(1)}, bf16[256,256]{1,0:T(8,128)(2,1)}, u32[]{:S(2)}) copy-start(bf16[256,256]{1,0:T(8,128)(2,1)} %w_first.1) | copy-start | bytes 393220
  41.9 44.0 %copy-start.2 = (bf16[256,256]{1,0:T(8,128)(2,1)S(1)}, bf16[256,256]{1,0:T(8,128)(2,1)}, u32[]{:S(2)}) copy-start(bf16[256,256]{1,0:T(8,128)(2,1)} %w_second.1) | copy-start | bytes 393220
  135.4 19.8 %all-to-all-start.4 = ((bf16[32,16,256]{2,1,0:T(8,128)(2,1)}), bf16[32,16,256]{2,1,0:T(8,128)(2,1)S(1)}, u32[]{:S(2)}, u32[]{:S(2)}) async-start(bf16[32,16,256]{2,1,0:T(8,128)(2,1)} %broadcast_in_dim.5), calls=%async_computation.4 | async-start | bytes 524288 | tf_op jit(solution)/shard_map/all_to_all | solution.py:137

commit v2 on v1

v2 whole, which is shorter than its diff:
```python
import jax
import jax.numpy as jnp
from jax import lax
from jax.experimental import pallas as pl
from jax.experimental.pallas import tpu as pltpu
from jax.sharding import PartitionSpec as P

TILE = 128
N_ROW = 16
N_COL = 32
SLOTS = 64
BLOCK = 1024
WIDTH = 256
USERS = BLOCK // N_COL
ITEMS = BLOCK // N_ROW
GRADS = 2 * WIDTH // N_COL
PEERS = N_COL // 2
HALF = BLOCK // 2
VMEM = pl.BlockSpec(memory_space=pltpu.VMEM)
SMEM = pl.BlockSpec(memory_space=pltpu.SMEM)
f32 = jnp.float32
bf16 = jnp.bfloat16


def params():
    return pltpu.CompilerParams(vmem_limit_bytes=40 * 1024 * 1024)


def cost(flops, moved):
    return pl.CostEstimate(flops=flops, bytes_accessed=moved, transcendentals=0)


def spread_kernel(features, cotangent, out):
    for i in range(N_ROW):
        out[i, :, :WIDTH] = features[...]
        out[i, :, WIDTH:] = cotangent[...]


def spread_items(features, cotangent):
    return pl.pallas_call(
        spread_kernel,
        out_shape=jax.ShapeDtypeStruct((N_ROW, ITEMS, 2 * WIDTH), bf16),
        in_specs=[VMEM, VMEM],
        out_specs=VMEM,
        compiler_params=params(),
        name="spread_items",
    )(features, cotangent)


def dense_kernel(core, ids, count, tiles, dense, turned):
    mine = core[0, 0]

    def place(k, carry):
        r = ids[0, k]
        c = pl.multiple_of(ids[1, k] * TILE, TILE)
        tile = jnp.where(k < count[0, 0], tiles[k], jnp.zeros((TILE, TILE), bf16))
        for part in range(TILE // USERS):
            half = lax.rem(part + mine, 2)
            row = pl.multiple_of(r * (TILE // 2) + part // 2 * USERS, USERS)
            dense[half, pl.ds(row, USERS), pl.ds(c, TILE)] = tile[part * USERS : (part + 1) * USERS]
        turned[pl.ds(c, TILE), pl.ds(pl.multiple_of(r * TILE, TILE), TILE)] = tile.T
        return carry

    lax.fori_loop(0, SLOTS, place, 0)


def make_dense(core, ids, count, tiles):
    return pl.pallas_call(
        dense_kernel,
        out_shape=(
            jax.ShapeDtypeStruct((2, HALF, BLOCK), bf16),
            jax.ShapeDtypeStruct((BLOCK, BLOCK), bf16),
        ),
        in_specs=[SMEM, SMEM, SMEM, VMEM],
        out_specs=(VMEM, VMEM),
        compiler_params=params(),
        cost_estimate=cost(0, 3 * 2 * BLOCK * BLOCK),
        name="dense_block",
    )(core, ids, count, tiles)


CHUNK = 256


def theirs_kernel(dense, items, out):
    for i in range(0, HALF, CHUNK):
        out[i : i + CHUNK] = jnp.dot(dense[1, i : i + CHUNK], items[...], preferred_element_type=f32).astype(bf16)


def mine_kernel(dense, items, other, out):
    for i in range(0, HALF, CHUNK):
        part = jnp.dot(dense[0, i : i + CHUNK], items[...], preferred_element_type=f32)
        out[i : i + CHUNK] = (part + other[i : i + CHUNK].astype(f32)).astype(bf16)


def half_product(kernel, *operands):
    return pl.pallas_call(
        kernel,
        out_shape=jax.ShapeDtypeStruct((HALF, 2 * WIDTH), bf16),
        in_specs=[VMEM] * len(operands),
        out_specs=VMEM,
        compiler_params=params(),
        cost_estimate=cost(2 * HALF * BLOCK * 2 * WIDTH, 3 * 1024 * 1024),
        name="user_product",
    )(*operands)


def middle_kernel(parts, w_first, w_second, out):
    total = parts[0].astype(f32)
    for i in range(1, PEERS):
        total = total + parts[i].astype(f32)
    sums = total[:, :WIDTH]
    d_users = total[:, WIDTH:].astype(bf16)
    high = sums.astype(bf16)
    low = (sums - high.astype(f32)).astype(bf16)
    w1 = w_first[...]
    w2 = w_second[...]
    z = jnp.dot(high, w1, preferred_element_type=f32) + jnp.dot(low, w1, preferred_element_type=f32)
    s = jax.nn.sigmoid(z)
    hidden = (z * s).astype(bf16)
    mapped = jnp.dot(hidden, w2, preferred_element_type=f32).astype(bf16)
    back = lax.dot_general(d_users, w2, (((1,), (1,)), ((), ())), preferred_element_type=f32)
    d_pre = (back * s * (1.0 + z * (1.0 - s))).astype(bf16)
    over_users = (((0,), (0,)), ((), ()))
    grad_one = lax.dot_general(high, d_pre, over_users, preferred_element_type=f32) + lax.dot_general(
        low, d_pre, over_users, preferred_element_type=f32
    )
    grad_two = lax.dot_general(hidden, d_users, over_users, preferred_element_type=f32)
    half = GRADS // 2
    for i in range(PEERS):
        out[i, :USERS] = mapped
        for k in range(2):
            rows = slice((2 * i + k) * half, (2 * i + k + 1) * half)
            both = jnp.concatenate([grad_one[rows], grad_two[rows]], axis=0)
            out[i, USERS + k * GRADS : USERS + (k + 1) * GRADS] = both.astype(bf16)


def middle(parts, w_first, w_second):
    return pl.pallas_call(
        middle_kernel,
        out_shape=jax.ShapeDtypeStruct((PEERS, USERS + 2 * GRADS, WIDTH), bf16),
        in_specs=[VMEM, VMEM, VMEM],
        out_specs=VMEM,
        compiler_params=params(),
        name="middle",
    )(parts, w_first, w_second)


def back_kernel(core, got, other, turned, out, mapped):
    mine = core[0, 0]
    slot = pl.multiple_of(USERS + mine * GRADS, GRADS)
    grads = jnp.zeros((GRADS, WIDTH), f32)
    for i in range(PEERS):
        grads = grads + got[i, pl.ds(slot, GRADS)].astype(f32) + other[i, pl.ds(slot, GRADS)].astype(f32)
        mapped[pl.ds(pl.multiple_of((2 * i + mine) * USERS, USERS), USERS)] = got[i, :USERS]
        mapped[pl.ds(pl.multiple_of((2 * i + 1 - mine) * USERS, USERS), USERS)] = other[i, :USERS]
    grads = grads.astype(bf16)
    for i in range(N_ROW):
        out[i, ITEMS:] = grads
    per = CHUNK // ITEMS
    for i in range(N_ROW // per):
        part = jnp.dot(turned[i * CHUNK : (i + 1) * CHUNK], mapped[...], preferred_element_type=f32).astype(bf16)
        for j in range(per):
            out[i * per + j, :ITEMS] = part[j * ITEMS : (j + 1) * ITEMS]


def back_product(core, got, other, turned):
    return pl.pallas_call(
        back_kernel,
        out_shape=jax.ShapeDtypeStruct((N_ROW, ITEMS + GRADS, WIDTH), bf16),
        in_specs=[SMEM, VMEM, VMEM, VMEM],
        out_specs=VMEM,
        scratch_shapes=[pltpu.VMEM((BLOCK, WIDTH), bf16)],
        compiler_params=params(),
        name="back_product",
    )(core, got, other, turned)


def shards(features, cotangent, w_first, w_second, adjacency_tiles, tile_ids, counts):
    core = lax.rem(lax.axis_index("col"), 2).reshape(1, 1)
    same_core = [[2 * i + k for i in range(PEERS)] for k in range(2)]
    swap = [(i, i ^ 1) for i in range(N_COL)]
    spread = spread_items(features, cotangent)
    dense, turned = make_dense(core, tile_ids[0, 0], counts, adjacency_tiles[0, 0])
    items = lax.all_to_all(spread, "row", 0, 0).reshape(BLOCK, 2 * WIDTH)
    other = lax.ppermute(half_product(theirs_kernel, dense, items), "col", swap)
    sums = half_product(mine_kernel, dense, items, other).reshape(PEERS, USERS, 2 * WIDTH)
    parts = lax.all_to_all(sums, "col", 0, 0, axis_index_groups=same_core)
    sent = middle(parts, w_first, w_second)
    got = lax.all_to_all(sent, "col", 0, 0, axis_index_groups=same_core)
    other = lax.ppermute(got, "col", swap)
    sent = back_product(core, got, other, turned)
    got = lax.all_to_all(sent, "row", 0, 0)
    grads = jnp.sum(got[:, ITEMS:].astype(f32), axis=0).astype(bf16)
    item_out = jnp.sum(got[:, :ITEMS].astype(f32), axis=0).astype(bf16)
    grads = lax.all_to_all(jnp.broadcast_to(grads[None], (N_COL, GRADS, WIDTH)), "col", 0, 0)
    half = GRADS // 2
    grad_one = grads[:, :half].astype(f32).reshape(WIDTH, WIDTH)
    grad_two = grads[:, half:].astype(f32).reshape(WIDTH, WIDTH)
    return (item_out, grad_one, grad_two)


def solution(mesh):
    return jax.shard_map(
        shards,
        mesh=mesh,
        in_specs=(
            P(("col", "row"), None),
            P(("col", "row"), None),
            P(),
            P(),
            P("row", "col", None, None, None),
            P("row", "col", None, None),
            P("row", "col"),
        ),
        out_specs=(P(("col", "row"), None), P(), P()),
        check_vma=False,
    )
```

time: 156 us -> 146 us (0.936)
  blocking collectives: 91.3 us -> 72.9 us
  starting transfers between devices: 21.7 us -> 27.1 us
  waiting for transfers between devices: 24.7 us -> 27.8 us
  matrix products: 2.86 us -> 0 us
  Pallas kernels: 6.9 us -> 9.25 us
    all_to_all x2, blocking collectives: 70.7 us -> 49.2 us  [the longest x1 29.4 us: shards(): parts = lax.all_to_all(sums, 'col', 0, 0, axis_index_groups=same_core)]
    ppermute x0 -> x2, starting transfers between devices: none -> 8.59 us  [the longest x1 4.4 us: shards(): other = lax.ppermute(got, 'col', swap)]
    all_to_all x1, starting transfers between devices: 8.32 us -> 5.11 us  [shards(): lax.all_to_all(jnp.broadcast_to(grads[None], (N_COL, GRADS, WIDTH)), 'col...]
    ppermute x0 -> x2, waiting for transfers between devices: none -> 3.03 us  [the longest x1 1.51 us: shards(): other = lax.ppermute(half_product(theirs_kernel, dense, items), 'col', swap)]
    all_to_all x1, blocking collectives: 20.7 us -> 23.6 us  [shards(): got = lax.all_to_all(sent, 'row', 0, 0)]
    dot_general x1 -> x0, matrix products: 2.86 us -> none  [shards(): partial = jnp.dot(dense, items, preferred_element_type=f32).astype(bf16)]
    pallas_call x2 -> x5, Pallas kernels: 6.18 us -> 8.49 us  [the longest x1 5.36 us: make_dense(): pl.pallas_call(dense_kernel, out_shape=(jax.ShapeDtypeStruct((2, HALF, BL...]
    unnamed x10 -> x16, local copies, waits for them, and re-layouts: 2.94 us -> 4.44 us
  transfers between devices with their start and end apart: 2 -> 4, of which waited for: 2 -> 4; matrix products, arithmetic and copies ran while one was open for 0% -> 0% of each run, Pallas kernels for 4% -> 4%
where the time goes in v2:
time: 146 us; the launch traced here: 145 us
  blocking collectives  72.9 us (50%)
  waiting for transfers between devices  27.8 us (19%)
  starting transfers between devices  27.1 us (19%)
  Pallas kernels  9.25 us (6%)
  local copies, waits for them, and re-layouts  5.17 us (4%)
  other arithmetic  1.54 us (1%)
    all_to_all x1, blocking collectives, shards(): parts = lax.all_to_all(sums, 'col', 0, 0, axis_index_groups=same_core)  29.4 us
    all_to_all x1, blocking collectives, shards(): got = lax.all_to_all(sent, 'row', 0, 0)  23.6 us
    all_to_all x1, blocking collectives, shards(): got = lax.all_to_all(sent, 'col', 0, 0, axis_index_groups=same_core)  19.9 us
    all_to_all x1, waiting for transfers between devices, shards(): items = lax.all_to_all(spread, 'row', 0, 0).reshape(BLOCK, 2 * WIDTH)  14.1 us
    all_to_all x1, starting transfers between devices, shards(): items = lax.all_to_all(spread, 'row', 0, 0).reshape(BLOCK, 2 * WIDTH)  13.4 us
    all_to_all x1, waiting for transfers between devices, shards(): lax.all_to_all(jnp.broadcast_to(grads[None], (N_COL, GRADS, WIDTH)), 'col...  10.7 us
    pallas_call x1, Pallas kernels, make_dense(): pl.pallas_call(dense_kernel, out_shape=(jax.ShapeDtypeStruct((2, HALF, BL...  5.36 us
    all_to_all x1, starting transfers between devices, shards(): lax.all_to_all(jnp.broadcast_to(grads[None], (N_COL, GRADS, WIDTH)), 'col...  5.11 us
  transfers between devices with their start and end apart: 4, of which 4 were waited for; matrix products, arithmetic and copies ran while one was open for 0% of the time, Pallas kernels for 4%

profile of v2, /device:TPU:1, one launch (start us, length us, event | category | flops | bytes accessed | tf_op | source)
XLA Modules:
  0.0 145.2 jit_solution(15823715385758336919)
XLA Ops:
  0.6 0.0 copy-start.5
  0.6 0.7 copy-done.5
  1.4 0.8 copy-done.6
  2.1 1.1 spread_items.1
  3.2 13.4 %all-to-all-start = ((bf16[16,64,512]{2,1,0:T(8,128)(2,1)}), bf16[16,64,512]{2,1,0:T(8,128)(2,1)S(1)}, u32[]{:S(2)}, u32[]{:S(2)}) async-start(bf16[16,64,512]{2,1,0:T(8,128)(2,1)} %spread_items.1), calls=%async_computation | async-start | bytes 2097152 | tf_op jit(solution)/shard_map/all_to_all | solution.py:185
  17.3 0.0 copy-done.7
  17.3 0.0 copy-start
  17.3 1.6 %copy-done = bf16[1,1,64,128,128]{4,3,2,1,0:T(8,128)(2,1)S(1)} copy-done((bf16[1,1,64,128,128]{4,3,2,1,0:T(8,128)(2,1)S(1)}, bf16[1,1,64,128,128]{4,3,2,1,0:T(8,128)(2,1)}, u32[]{:S(2)}) %copy-start) | copy-done | bytes 2097176
  18.9 5.4 %dense_block.1 = (bf16[2,512,1024]{2,1,0:T(8,128)(2,1)S(1)}, bf16[1024,1024]{1,0:T(8,128)(2,1)S(1)}) custom-call(s32[1,1]{1,0:T(1,128)} %bitcast.core, s32[2,64]{1,0:T(2,128)S(1)} %bitcast.19, s32[1,1]{1,0:T(1,128)S(6)} %copy.10.count, bf16[64,128,128]{2,1,0:T(8,128)(2,1)S(1)} %bitcast.17), custom_call_target="tpu_custom_call" | custom-call | bytes 6291456 | tf_op jit(solution)/shard_map/dense_block/pallas_call | solution.py:68
  24.3 0.0 copy-start.1
  24.3 1.3 copy-done.1
  25.6 14.1 %all-to-all-done = bf16[16,64,512]{2,1,0:T(8,128)(2,1)S(1)} async-done(((bf16[16,64,512]{2,1,0:T(8,128)(2,1)}), bf16[16,64,512]{2,1,0:T(8,128)(2,1)S(1)}, u32[]{:S(2)}, u32[]{:S(2)}) %all-to-all-start) | async-done | bytes 1048608 | tf_op jit(solution)/shard_map/all_to_all | solution.py:185
  39.7 0.7 user_product.2
  40.4 0.0 copy-start.3
  40.4 0.0 copy-start.4
  40.4 4.2 %collective-permute-start = (bf16[512,512]{1,0:T(8,128)(2,1)S(1)}, bf16[512,512]{1,0:T(8,128)(2,1)S(1)}, u32[]{:S(2)}, u32[]{:S(2)}) collective-permute-start(bf16[512,512]{1,0:T(8,128)(2,1)S(1)} %user_product.2), channel_id=1, source_target_pairs={{0,1},{1,0},{2,3},{3,2},{4,5},{5,4},{6,7},{7,6},{8,9},{9,8},{10,11... | collective-permute-start | bytes 1572872 | tf_op jit(solution)/shard_map/ppermute | solution.py:186
  44.6 1.5 %collective-permute-done.other = bf16[512,512]{1,0:T(8,128)(2,1)S(1)} collective-permute-done((bf16[512,512]{1,0:T(8,128)(2,1)S(1)}, bf16[512,512]{1,0:T(8,128)(2,1)S(1)}, u32[]{:S(2)}, u32[]{:S(2)}) %collective-permute-start) | collective-permute-done | bytes 524320 | tf_op jit(solution)/shard_map/ppermute | solution.py:186
  46.1 0.7 user_product.3
  46.9 0.0 copy-start.2
  46.9 29.4 %all_to_all.25.parts = bf16[16,32,512]{2,1,0:T(8,128)(2,1)S(1)} all-to-all(bf16[16,32,512]{2,1,0:T(8,128)(2,1)S(1)} %bitcast.18), channel_id=1, replica_groups={{0,2,4,6,8,10,12,14,16,18,20,22,24,26,28,30},{1,3,5,7,9,11,13,15,17,19,..., dimensions={0} | all-to-all | bytes 1048576 | tf_op jit(solution)/shard_map/all_to_all | solution.py:188
  76.3 0.0 copy-done.4
  76.3 0.6 middle.1
  76.9 19.9 %all_to_all.26.got = bf16[16,64,256]{2,1,0:T(8,128)(2,1)S(1)} all-to-all(bf16[16,64,256]{2,1,0:T(8,128)(2,1)S(1)} %middle.1), channel_id=1, replica_groups={{0,2,4,6,8,10,12,14,16,18,20,22,24,26,28,30},{1,3,5,7,9,11,13,15,17,19,..., dimensions={0} | all-to-all | bytes 1048576 | tf_op jit(solution)/shard_map/all_to_all | solution.py:190
  96.8 4.4 %collective-permute-start.1 = (bf16[16,64,256]{2,1,0:T(8,128)(2,1)S(1)}, bf16[16,64,256]{2,1,0:T(8,128)(2,1)S(1)}, u32[]{:S(2)}, u32[]{:S(2)}) collective-permute-start(bf16[16,64,256]{2,1,0:T(8,128)(2,1)S(1)} %all_to_all.26.got), channel_id=1, source_target_pairs={{0,1},{1,0},{2,3},{3,2},{4,5},{5,4},{6,7},{7,6},{8,9},{9,8},{10,11... | collective-permute-start | bytes 1572872 | tf_op jit(solution)/shard_map/ppermute | solution.py:191
  101.2 1.5 %collective-permute-done.1.other = bf16[16,64,256]{2,1,0:T(8,128)(2,1)S(1)} collective-permute-done((bf16[16,64,256]{2,1,0:T(8,128)(2,1)S(1)}, bf16[16,64,256]{2,1,0:T(8,128)(2,1)S(1)}, u32[]{:S(2)}, u32[]{:S(2)}) %collective-permute-start.1) | collective-permute-done | bytes 524320 | tf_op jit(solution)/shard_map/ppermute | solution.py:191
  102.7 0.8 back_product.1
  103.5 23.6 %all_to_all.27 = bf16[16,80,256]{2,1,0:T(8,128)(2,1)S(1)} all-to-all(bf16[16,80,256]{2,1,0:T(8,128)(2,1)S(1)} %back_product.1), channel_id=1, replica_groups=mesh['row'=16,'col'=32] {'row'}, dimensions={0} | all-to-all | bytes 1310720 | tf_op jit(solution)/shard_map/all_to_all | solution.py:193
  127.1 0.7 broadcast_in_dim.2
  127.9 5.1 %all-to-all-start.4 = ((bf16[32,16,256]{2,1,0:T(8,128)(2,1)}), bf16[32,16,256]{2,1,0:T(8,128)(2,1)S(1)}, u32[]{:S(2)}, u32[]{:S(2)}) async-start(bf16[32,16,256]{2,1,0:T(8,128)(2,1)} %broadcast_in_dim.2), calls=%async_computation.4 | async-start | bytes 524288 | tf_op jit(solution)/shard_map/all_to_all | solution.py:196
  133.0 0.7 slice_reduce_fusion
  133.7 10.7 %all-to-all-done.4 = bf16[32,16,256]{2,1,0:T(8,128)(2,1)S(1)} async-done(((bf16[32,16,256]{2,1,0:T(8,128)(2,1)}), bf16[32,16,256]{2,1,0:T(8,128)(2,1)S(1)}, u32[]{:S(2)}, u32[]{:S(2)}) %all-to-all-start.4) | async-done | bytes 262176 | tf_op jit(solution)/shard_map/all_to_all | solution.py:196
  144.4 0.8 fusion
  (5 shorter events, 0.0 us)
Async XLA Ops:
  0.6 0.8 copy-start.5
  1.4 0.8 copy-start.6
  2.1 15.2 %copy-start.7 = (s32[1,1,2,64]{3,2,1,0:T(2,128)S(1)}, s32[1,1,2,64]{3,2,1,0:T(2,128)}, u32[]{:S(2)}) copy-start(s32[1,1,2,64]{3,2,1,0:T(2,128)} %param.12) | copy-start | bytes 1540
  3.2 36.5 %all-to-all-start = ((bf16[16,64,512]{2,1,0:T(8,128)(2,1)}), bf16[16,64,512]{2,1,0:T(8,128)(2,1)S(1)}, u32[]{:S(2)}, u32[]{:S(2)}) async-start(bf16[16,64,512]{2,1,0:T(8,128)(2,1)} %spread_items.1), calls=%async_computation | async-start | bytes 2097152 | tf_op jit(solution)/shard_map/all_to_all | solution.py:185
  17.3 1.6 %copy-start = (bf16[1,1,64,128,128]{4,3,2,1,0:T(8,128)(2,1)S(1)}, bf16[1,1,64,128,128]{4,3,2,1,0:T(8,128)(2,1)}, u32[]{:S(2)}) copy-start(bf16[1,1,64,128,128]{4,3,2,1,0:T(8,128)(2,1)} %param.11) | copy-start | bytes 6291460
  24.3 1.3 copy-start.1
  40.4 35.8 %copy-start.3 = (bf16[256,256]{1,0:T(8,128)(2,1)S(1)}, bf16[256,256]{1,0:T(8,128)(2,1)}, u32[]{:S(2)}) copy-start(bf16[256,256]{1,0:T(8,128)(2,1)} %w_first.1) | copy-start | bytes 393220
  40.4 35.8 %copy-start.4 = (bf16[256,256]{1,0:T(8,128)(2,1)S(1)}, bf16[256,256]{1,0:T(8,128)(2,1)}, u32[]{:S(2)}) copy-start(bf16[256,256]{1,0:T(8,128)(2,1)} %w_second.1) | copy-start | bytes 393220
  40.4 5.7 %collective-permute-start = (bf16[512,512]{1,0:T(8,128)(2,1)S(1)}, bf16[512,512]{1,0:T(8,128)(2,1)S(1)}, u32[]{:S(2)}, u32[]{:S(2)}) collective-permute-start(bf16[512,512]{1,0:T(8,128)(2,1)S(1)} %user_product.2), channel_id=1, source_target_pairs={{0,1},{1,0},{2,3},{3,2},{4,5},{5,4},{6,7},{7,6},{8,9},{9,8},{10,11... | collective-permute-start | bytes 1572872 | tf_op jit(solution)/shard_map/ppermute | solution.py:186
  46.9 55.8 %copy-start.2 = (bf16[1024,1024]{1,0:T(8,128)(2,1)S(1)}, bf16[1024,1024]{1,0:T(8,128)(2,1)}, u32[]{:S(2)}) copy-start(bf16[1024,1024]{1,0:T(8,128)(2,1)} %copy-done.1) | copy-start | bytes 6291460
  96.8 5.9 %collective-permute-start.1 = (bf16[16,64,256]{2,1,0:T(8,128)(2,1)S(1)}, bf16[16,64,256]{2,1,0:T(8,128)(2,1)S(1)}, u32[]{:S(2)}, u32[]{:S(2)}) collective-permute-start(bf16[16,64,256]{2,1,0:T(8,128)(2,1)S(1)} %all_to_all.26.got), channel_id=1, source_target_pairs={{0,1},{1,0},{2,3},{3,2},{4,5},{5,4},{6,7},{7,6},{8,9},{9,8},{10,11... | collective-permute-start | bytes 1572872 | tf_op jit(solution)/shard_map/ppermute | solution.py:191
  127.9 16.6 %all-to-all-start.4 = ((bf16[32,16,256]{2,1,0:T(8,128)(2,1)}), bf16[32,16,256]{2,1,0:T(8,128)(2,1)S(1)}, u32[]{:S(2)}, u32[]{:S(2)}) async-start(bf16[32,16,256]{2,1,0:T(8,128)(2,1)} %broadcast_in_dim.2), calls=%async_computation.4 | async-start | bytes 524288 | tf_op jit(solution)/shard_map/all_to_all | solution.py:196

commit v3 on v2

--- a/solution.py
+++ b/solution.py
@@ -15,53 +15,99 @@
 ITEMS = BLOCK // N_ROW
 GRADS = 2 * WIDTH // N_COL
 PEERS = N_COL // 2
+NEAR = 4
 HALF = BLOCK // 2
 VMEM = pl.BlockSpec(memory_space=pltpu.VMEM)
+ANY = pl.BlockSpec(memory_space=pl.ANY)
 SMEM = pl.BlockSpec(memory_space=pltpu.SMEM)
 f32 = jnp.float32
 bf16 = jnp.bfloat16
 
 
-def params():
-    return pltpu.CompilerParams(vmem_limit_bytes=40 * 1024 * 1024)
+def params(mib=24):
+    return pltpu.CompilerParams(vmem_limit_bytes=mib * 1024 * 1024)
 
 
 def cost(flops, moved):
     return pl.CostEstimate(flops=flops, bytes_accessed=moved, transcendentals=0)
 
 
-def spread_kernel(features, cotangent, out):
-    for i in range(N_ROW):
-        out[i, :, :WIDTH] = features[...]
-        out[i, :, WIDTH:] = cotangent[...]
-
-
-def spread_items(features, cotangent):
-    return pl.pallas_call(
-        spread_kernel,
-        out_shape=jax.ShapeDtypeStruct((N_ROW, ITEMS, 2 * WIDTH), bf16),
-        in_specs=[VMEM, VMEM],
-        out_specs=VMEM,
-        compiler_params=params(),
-        name="spread_items",
-    )(features, cotangent)
-
-
-def dense_kernel(core, ids, count, tiles, dense, turned):
+def held(array):
+    return pltpu.with_memory_space_constraint(array, pltpu.HBM)
+
+
+def first_kernel(features, cotangent, out, both, in_sems, out_sems):
+    loads = [
+        pltpu.make_async_copy(features, both.at[:, :WIDTH], in_sems.at[0]),
+        pltpu.make_async_copy(cotangent, both.at[:, WIDTH:], in_sems.at[1]),
+    ]
+    for copy in loads:
+        copy.start()
+    for copy in loads:
+        copy.wait()
+    stores = [pltpu.make_async_copy(both, out.at[i], out_sems.at[i]) for i in range(NEAR)]
+    for copy in stores:
+        copy.start()
+    for copy in stores:
+        copy.wait()
+
+
+def first_spread(features, cotangent):
+    return pl.pallas_call(
+        first_kernel,
+        out_shape=jax.ShapeDtypeStruct((NEAR, ITEMS, 2 * WIDTH), bf16),
+        in_specs=[ANY, ANY],
+        out_specs=ANY,
+        scratch_shapes=[
+            pltpu.VMEM((ITEMS, 2 * WIDTH), bf16),
+            pltpu.SemaphoreType.DMA((2,)),
+            pltpu.SemaphoreType.DMA((NEAR,)),
+        ],
+        compiler_params=params(),
+        cost_estimate=cost(0, 2 * NEAR * ITEMS * 4 * WIDTH),
+        name="first_spread",
+    )(held(features), held(cotangent))
+
+
+def second_kernel(rows, after, out):
+    for i in range(NEAR):
+        out[i] = rows[...]
+
+
+def second_spread(rows, after):
+    return pl.pallas_call(
+        second_kernel,
+        out_shape=jax.ShapeDtypeStruct((NEAR,) + rows.shape, bf16),
+        in_specs=[VMEM, ANY],
+        out_specs=VMEM,
+        compiler_params=params(),
+        name="second_spread",
+    )(rows, after)
+
+
+LOADS = 8
+LOAD = SLOTS // LOADS
+
+
+def dense_kernel(core, ids, count, tiles, dense, turned, held, sems):
     mine = core[0, 0]
-
-    def place(k, carry):
-        r = ids[0, k]
-        c = pl.multiple_of(ids[1, k] * TILE, TILE)
-        tile = jnp.where(k < count[0, 0], tiles[k], jnp.zeros((TILE, TILE), bf16))
-        for part in range(TILE // USERS):
-            half = lax.rem(part + mine, 2)
-            row = pl.multiple_of(r * (TILE // 2) + part // 2 * USERS, USERS)
-            dense[half, pl.ds(row, USERS), pl.ds(c, TILE)] = tile[part * USERS : (part + 1) * USERS]
-        turned[pl.ds(c, TILE), pl.ds(pl.multiple_of(r * TILE, TILE), TILE)] = tile.T
-        return carry
-
-    lax.fori_loop(0, SLOTS, place, 0)
+    copies = []
+    for i in range(LOADS):
+        part = pl.ds(i * LOAD, LOAD)
+        copies.append(pltpu.make_async_copy(tiles.at[part], held.at[part], sems.at[i]))
+    for copy in copies:
+        copy.start()
+    for i in range(LOADS):
+        copies[i].wait()
+        for k in range(i * LOAD, (i + 1) * LOAD):
+            r = ids[0, k]
+            c = pl.multiple_of(ids[1, k] * TILE, TILE)
+            tile = jnp.where(k < count[0, 0], held[k], jnp.zeros((TILE, TILE), bf16))
+            for part in range(TILE // USERS):
+                half = lax.rem(part + mine, 2)
+                row = pl.multiple_of(r * (TILE // 2) + part // 2 * USERS, USERS)
+                dense[half, pl.ds(row, USERS), pl.ds(c, TILE)] = tile[part * USERS : (part + 1) * USERS]
+            turned[pl.ds(c, TILE), pl.ds(pl.multiple_of(r * TILE, TILE), TILE)] = tile.T
 
 
 def make_dense(core, ids, count, tiles):
@@ -71,12 +117,13 @@
             jax.ShapeDtypeStruct((2, HALF, BLOCK), bf16),
             jax.ShapeDtypeStruct((BLOCK, BLOCK), bf16),
         ),
-        in_specs=[SMEM, SMEM, SMEM, VMEM],
+        in_specs=[SMEM, SMEM, SMEM, ANY],
         out_specs=(VMEM, VMEM),
+        scratch_shapes=[pltpu.VMEM((SLOTS, TILE, TILE), bf16), pltpu.SemaphoreType.DMA((LOADS,))],
         compiler_params=params(),
         cost_estimate=cost(0, 3 * 2 * BLOCK * BLOCK),
         name="dense_block",
-    )(core, ids, count, tiles)
+    )(core, ids, count, held(tiles))
 
 
 CHUNK = 256
@@ -176,13 +223,36 @@
     )(core, got, other, turned)
 
 
+def last_kernel(got, out):
+    grads = got[0, ITEMS:].astype(f32)
+    for i in range(1, N_ROW):
+        grads = grads + got[i, ITEMS:].astype(f32)
+    grads = grads.astype(bf16)
+    for i in range(N_COL):
+        out[i] = grads
+
+
+def last_spread(got):
+    return pl.pallas_call(
+        last_kernel,
+        out_shape=jax.ShapeDtypeStruct((N_COL, GRADS, WIDTH), bf16),
+        in_specs=[VMEM],
+        out_specs=VMEM,
+        compiler_params=params(),
+        name="last_spread",
+    )(got)
+
+
 def shards(features, cotangent, w_first, w_second, adjacency_tiles, tile_ids, counts):
     core = lax.rem(lax.axis_index("col"), 2).reshape(1, 1)
     same_core = [[2 * i + k for i in range(PEERS)] for k in range(2)]
     swap = [(i, i ^ 1) for i in range(N_COL)]
-    spread = spread_items(features, cotangent)
+    same_x = [[NEAR * i + k for k in range(NEAR)] for i in range(NEAR)]
+    same_z = [[NEAR * i + k for i in range(NEAR)] for k in range(NEAR)]
+    spread = first_spread(features, cotangent)
     dense, turned = make_dense(core, tile_ids[0, 0], counts, adjacency_tiles[0, 0])
-    items = lax.all_to_all(spread, "row", 0, 0).reshape(BLOCK, 2 * WIDTH)
+    items = lax.all_to_all(spread, "row", 0, 0, axis_index_groups=same_x).reshape(NEAR * ITEMS, 2 * WIDTH)
+    items = lax.all_to_all(second_spread(items, dense), "row", 0, 0, axis_index_groups=same_z).reshape(BLOCK, 2 * WIDTH)
     other = lax.ppermute(half_product(theirs_kernel, dense, items), "col", swap)
     sums = half_product(mine_kernel, dense, items, other).reshape(PEERS, USERS, 2 * WIDTH)
     parts = lax.all_to_all(sums, "col", 0, 0, axis_index_groups=same_core)
@@ -191,9 +261,8 @@
     other = lax.ppermute(got, "col", swap)
     sent = back_product(core, got, other, turned)
     got = lax.all_to_all(sent, "row", 0, 0)
-    grads = jnp.sum(got[:, ITEMS:].astype(f32), axis=0).astype(bf16)
     item_out = jnp.sum(got[:, :ITEMS].astype(f32), axis=0).astype(bf16)
-    grads = lax.all_to_all(jnp.broadcast_to(grads[None], (N_COL, GRADS, WIDTH)), "col", 0, 0)
+    grads = lax.all_to_all(last_spread(got), "col", 0, 0)
     half = GRADS // 2
     grad_one = grads[:, :half].astype(f32).reshape(WIDTH, WIDTH)
     grad_two = grads[:, half:].astype(f32).reshape(WIDTH, WIDTH)

time: 146 us -> 141 us (0.966)
  waiting for transfers between devices: 27.8 us -> 16 us
  blocking collectives: 72.9 us -> 83.5 us
  local copies, waits for them, and re-layouts: 5.17 us -> 2.02 us
    all_to_all x0 -> x1, blocking collectives: none -> 14.4 us  [shards(): lax.all_to_all(second_spread(items, dense), 'row', 0, 0, axis_index_group...]
    all_to_all x2, waiting for transfers between devices: 24.8 us -> 13 us  [the longest x1 10.7 us: shards(): grads = lax.all_to_all(last_spread(got), 'col', 0, 0)]
    all_to_all x1, blocking collectives: 29.4 us -> 25.8 us  [shards(): parts = lax.all_to_all(sums, 'col', 0, 0, axis_index_groups=same_core)]
    ppermute x1, starting transfers between devices: 4.19 us -> 7.47 us  [shards(): other = lax.ppermute(half_product(theirs_kernel, dense, items), 'col', swap)]
    all_to_all x2, starting transfers between devices: 18.5 us -> 16 us  [the longest x1 10.9 us: shards(): lax.all_to_all(spread, 'row', 0, 0, axis_index_groups=same_x)]
    unnamed x16 -> x10, local copies, waits for them, and re-layouts: 4.44 us -> 2.02 us
    pallas_call x1, Pallas kernels: 5.36 us -> 3.19 us  [make_dense(): pl.pallas_call(dense_kernel, out_shape=(jax.ShapeDtypeStruct((2, HALF, BL...]
  transfers between devices with their start and end apart: 4 -> 4, of which waited for: 4 -> 4; matrix products, arithmetic and copies ran while one was open for 0% -> 0% of each run, Pallas kernels for 4% -> 2%
where the time goes in v3:
time: 141 us
  blocking collectives  83.5 us (59%)
  starting transfers between devices  27.9 us (20%)
  waiting for transfers between devices  16 us (11%)
  Pallas kernels  8.33 us (6%)
  local copies, waits for them, and re-layouts  2.02 us (1%)
  other arithmetic  1.51 us (1%)
    all_to_all x1, blocking collectives, shards(): parts = lax.all_to_all(sums, 'col', 0, 0, axis_index_groups=same_core)  25.8 us
    all_to_all x1, blocking collectives, shards(): got = lax.all_to_all(sent, 'row', 0, 0)  23.3 us
    all_to_all x1, blocking collectives, shards(): got = lax.all_to_all(sent, 'col', 0, 0, axis_index_groups=same_core)  19.9 us
    all_to_all x1, blocking collectives, shards(): lax.all_to_all(second_spread(items, dense), 'row', 0, 0, axis_index_group...  14.4 us
    all_to_all x1, starting transfers between devices, shards(): lax.all_to_all(spread, 'row', 0, 0, axis_index_groups=same_x)  10.9 us
    all_to_all x1, waiting for transfers between devices, shards(): grads = lax.all_to_all(last_spread(got), 'col', 0, 0)  10.7 us
    ppermute x1, starting transfers between devices, shards(): other = lax.ppermute(half_product(theirs_kernel, dense, items), 'col', swap)  7.47 us
    all_to_all x1, starting transfers between devices, shards(): grads = lax.all_to_all(last_spread(got), 'col', 0, 0)  5.12 us
  transfers between devices with their start and end apart: 4, of which 4 were waited for; matrix products, arithmetic and copies ran while one was open for 0% of the time, Pallas kernels for 2%

profile of v3, /device:TPU:1, one launch (start us, length us, event | category | flops | bytes accessed | tf_op | source)
XLA Modules:
  0.0 140.7 jit_solution(3905055159733859977)
XLA Ops:
  0.6 1.5 %first_spread.1 = bf16[4,64,512]{2,1,0:T(8,128)(2,1)} custom-call(bf16[64,256]{1,0:T(8,128)(2,1)} %features.1, bf16[64,256]{1,0:T(8,128)(2,1)} %cotangent.1), custom_call_target="tpu_custom_call" | custom-call | bytes 524288 | tf_op jit(solution)/shard_map/first_spread/pallas_call | solution.py:56
  2.2 10.9 %all-to-all-start = ((bf16[4,64,512]{2,1,0:T(8,128)(2,1)}), bf16[4,64,512]{2,1,0:T(8,128)(2,1)S(1)}, u32[]{:S(2)}, u32[]{:S(2)}) async-start(bf16[4,64,512]{2,1,0:T(8,128)(2,1)} %first_spread.1), calls=%async_computation | async-start | bytes 524288 | tf_op jit(solution)/shard_map/all_to_all | solution.py:254
  13.7 0.0 copy-start.4
  13.7 0.7 copy-done.4
  14.3 3.2 %dense_block.1 = (bf16[2,512,1024]{2,1,0:T(8,128)(2,1)S(1)}, bf16[1024,1024]{1,0:T(8,128)(2,1)S(1)}) custom-call(s32[1,1]{1,0:T(1,128)} %bitcast.core, s32[2,64]{1,0:T(2,128)S(1)} %bitcast.20, s32[1,1]{1,0:T(1,128)S(6)} %copy.10.count, bf16[64,128,128]{2,1,0:T(8,128)(2,1)} %bitcast.21), custom_call_target="tpu_custom_call" | custom-call | bytes 6291456 | tf_op jit(solution)/shard_map/dense_block/pallas_call | solution.py:114
  17.5 0.0 copy-start
  17.6 1.3 copy-done
  18.9 2.3 %all-to-all-done = bf16[4,64,512]{2,1,0:T(8,128)(2,1)S(1)} async-done(((bf16[4,64,512]{2,1,0:T(8,128)(2,1)}), bf16[4,64,512]{2,1,0:T(8,128)(2,1)S(1)}, u32[]{:S(2)}, u32[]{:S(2)}) %all-to-all-start) | async-done | bytes 262176 | tf_op jit(solution)/shard_map/all_to_all | solution.py:254
  21.2 0.1 second_spread.1
  21.2 14.4 %all_to_all.30 = bf16[4,256,512]{2,1,0:T(8,128)(2,1)S(1)} all-to-all(bf16[4,256,512]{2,1,0:T(8,128)(2,1)S(1)} %second_spread.1), channel_id=1, replica_groups={{0,128,256,384},{32,160,288,416},{64,192,320,448},{96,224,352,480},{1,1..., dimensions={0} | all-to-all | bytes 2097152 | tf_op jit(solution)/shard_map/all_to_all | solution.py:255
  35.7 0.7 user_product.2
  36.4 0.0 copy-start.2
  36.4 0.0 copy-start.3
  36.4 7.5 %collective-permute-start = (bf16[512,512]{1,0:T(8,128)(2,1)S(1)}, bf16[512,512]{1,0:T(8,128)(2,1)S(1)}, u32[]{:S(2)}, u32[]{:S(2)}) collective-permute-start(bf16[512,512]{1,0:T(8,128)(2,1)S(1)} %user_product.2), channel_id=1, source_target_pairs={{0,1},{1,0},{2,3},{3,2},{4,5},{5,4},{6,7},{7,6},{8,9},{9,8},{10,11... | collective-permute-start | bytes 1572872 | tf_op jit(solution)/shard_map/ppermute | solution.py:256
  43.9 1.5 %collective-permute-done.other = bf16[512,512]{1,0:T(8,128)(2,1)S(1)} collective-permute-done((bf16[512,512]{1,0:T(8,128)(2,1)S(1)}, bf16[512,512]{1,0:T(8,128)(2,1)S(1)}, u32[]{:S(2)}, u32[]{:S(2)}) %collective-permute-start) | collective-permute-done | bytes 524320 | tf_op jit(solution)/shard_map/ppermute | solution.py:256
  45.4 0.7 user_product.3
  46.1 0.0 copy-start.1
  46.1 25.8 %all_to_all.31.parts = bf16[16,32,512]{2,1,0:T(8,128)(2,1)S(1)} all-to-all(bf16[16,32,512]{2,1,0:T(8,128)(2,1)S(1)} %bitcast.18), channel_id=1, replica_groups={{0,2,4,6,8,10,12,14,16,18,20,22,24,26,28,30},{1,3,5,7,9,11,13,15,17,19,..., dimensions={0} | all-to-all | bytes 1048576 | tf_op jit(solution)/shard_map/all_to_all | solution.py:258
  71.9 0.0 copy-done.2
  71.9 0.0 copy-done.3
  72.0 0.6 middle.1
  72.6 19.9 %all_to_all.32.got = bf16[16,64,256]{2,1,0:T(8,128)(2,1)S(1)} all-to-all(bf16[16,64,256]{2,1,0:T(8,128)(2,1)S(1)} %middle.1), channel_id=1, replica_groups={{0,2,4,6,8,10,12,14,16,18,20,22,24,26,28,30},{1,3,5,7,9,11,13,15,17,19,..., dimensions={0} | all-to-all | bytes 1048576 | tf_op jit(solution)/shard_map/all_to_all | solution.py:260
  92.5 4.4 %collective-permute-start.1 = (bf16[16,64,256]{2,1,0:T(8,128)(2,1)S(1)}, bf16[16,64,256]{2,1,0:T(8,128)(2,1)S(1)}, u32[]{:S(2)}, u32[]{:S(2)}) collective-permute-start(bf16[16,64,256]{2,1,0:T(8,128)(2,1)S(1)} %all_to_all.32.got), channel_id=1, source_target_pairs={{0,1},{1,0},{2,3},{3,2},{4,5},{5,4},{6,7},{7,6},{8,9},{9,8},{10,11... | collective-permute-start | bytes 1572872 | tf_op jit(solution)/shard_map/ppermute | solution.py:261
  96.9 1.5 %collective-permute-done.1.other = bf16[16,64,256]{2,1,0:T(8,128)(2,1)S(1)} collective-permute-done((bf16[16,64,256]{2,1,0:T(8,128)(2,1)S(1)}, bf16[16,64,256]{2,1,0:T(8,128)(2,1)S(1)}, u32[]{:S(2)}, u32[]{:S(2)}) %collective-permute-start.1) | collective-permute-done | bytes 524320 | tf_op jit(solution)/shard_map/ppermute | solution.py:261
  98.4 0.0 copy-done.1
  98.5 0.8 back_product.1
  99.2 23.3 %all_to_all.33.got = bf16[16,80,256]{2,1,0:T(8,128)(2,1)S(1)} all-to-all(bf16[16,80,256]{2,1,0:T(8,128)(2,1)S(1)} %back_product.1), channel_id=1, replica_groups=mesh['row'=16,'col'=32] {'row'}, dimensions={0} | all-to-all | bytes 1310720 | tf_op jit(solution)/shard_map/all_to_all | solution.py:263
  122.6 0.7 last_spread.1
  123.3 5.1 %all-to-all-start.5 = ((bf16[32,16,256]{2,1,0:T(8,128)(2,1)}), bf16[32,16,256]{2,1,0:T(8,128)(2,1)S(1)}, u32[]{:S(2)}, u32[]{:S(2)}) async-start(bf16[32,16,256]{2,1,0:T(8,128)(2,1)} %last_spread.1), calls=%async_computation.5 | async-start | bytes 524288 | tf_op jit(solution)/shard_map/all_to_all | solution.py:265
  128.4 0.7 slice_reduce_fusion
  129.1 10.7 %all-to-all-done.5 = bf16[32,16,256]{2,1,0:T(8,128)(2,1)S(1)} async-done(((bf16[32,16,256]{2,1,0:T(8,128)(2,1)}), bf16[32,16,256]{2,1,0:T(8,128)(2,1)S(1)}, u32[]{:S(2)}, u32[]{:S(2)}) %all-to-all-start.5) | async-done | bytes 262176 | tf_op jit(solution)/shard_map/all_to_all | solution.py:265
  139.9 0.8 fusion
Async XLA Ops:
  2.2 19.0 %all-to-all-start = ((bf16[4,64,512]{2,1,0:T(8,128)(2,1)}), bf16[4,64,512]{2,1,0:T(8,128)(2,1)S(1)}, u32[]{:S(2)}, u32[]{:S(2)}) async-start(bf16[4,64,512]{2,1,0:T(8,128)(2,1)} %first_spread.1), calls=%async_computation | async-start | bytes 524288 | tf_op jit(solution)/shard_map/all_to_all | solution.py:254
  13.7 0.7 copy-start.4
  17.5 1.3 copy-start
  36.4 35.6 %copy-start.2 = (bf16[256,256]{1,0:T(8,128)(2,1)S(1)}, bf16[256,256]{1,0:T(8,128)(2,1)}, u32[]{:S(2)}) copy-start(bf16[256,256]{1,0:T(8,128)(2,1)} %w_first.1) | copy-start | bytes 393220
  36.4 35.6 %copy-start.3 = (bf16[256,256]{1,0:T(8,128)(2,1)S(1)}, bf16[256,256]{1,0:T(8,128)(2,1)}, u32[]{:S(2)}) copy-start(bf16[256,256]{1,0:T(8,128)(2,1)} %w_second.1) | copy-start | bytes 393220
  36.4 9.0 %collective-permute-start = (bf16[512,512]{1,0:T(8,128)(2,1)S(1)}, bf16[512,512]{1,0:T(8,128)(2,1)S(1)}, u32[]{:S(2)}, u32[]{:S(2)}) collective-permute-start(bf16[512,512]{1,0:T(8,128)(2,1)S(1)} %user_product.2), channel_id=1, source_target_pairs={{0,1},{1,0},{2,3},{3,2},{4,5},{5,4},{6,7},{7,6},{8,9},{9,8},{10,11... | collective-permute-start | bytes 1572872 | tf_op jit(solution)/shard_map/ppermute | solution.py:256
  46.1 52.4 %copy-start.1 = (bf16[1024,1024]{1,0:T(8,128)(2,1)S(1)}, bf16[1024,1024]{1,0:T(8,128)(2,1)}, u32[]{:S(2)}) copy-start(bf16[1024,1024]{1,0:T(8,128)(2,1)} %copy-done) | copy-start | bytes 6291460
  92.5 5.9 %collective-permute-start.1 = (bf16[16,64,256]{2,1,0:T(8,128)(2,1)S(1)}, bf16[16,64,256]{2,1,0:T(8,128)(2,1)S(1)}, u32[]{:S(2)}, u32[]{:S(2)}) collective-permute-start(bf16[16,64,256]{2,1,0:T(8,128)(2,1)S(1)} %all_to_all.32.got), channel_id=1, source_target_pairs={{0,1},{1,0},{2,3},{3,2},{4,5},{5,4},{6,7},{7,6},{8,9},{9,8},{10,11... | collective-permute-start | bytes 1572872 | tf_op jit(solution)/shard_map/ppermute | solution.py:261
  123.3 16.6 %all-to-all-start.5 = ((bf16[32,16,256]{2,1,0:T(8,128)(2,1)}), bf16[32,16,256]{2,1,0:T(8,128)(2,1)S(1)}, u32[]{:S(2)}, u32[]{:S(2)}) async-start(bf16[32,16,256]{2,1,0:T(8,128)(2,1)} %last_spread.1), calls=%async_computation.5 | async-start | bytes 524288 | tf_op jit(solution)/shard_map/all_to_all | solution.py:265

commit v4 on v3

--- a/solution.py
+++ b/solution.py
@@ -16,6 +16,8 @@
 GRADS = 2 * WIDTH // N_COL
 PEERS = N_COL // 2
 NEAR = 4
+RING = (0, 7, 1, 6, 2, 5, 3, 4)
+COLS = tuple(2 * y + half for half in range(2) for y in RING)
 HALF = BLOCK // 2
 VMEM = pl.BlockSpec(memory_space=pltpu.VMEM)
 ANY = pl.BlockSpec(memory_space=pl.ANY)
@@ -89,41 +91,65 @@
 LOAD = SLOTS // LOADS
 
 
-def dense_kernel(core, ids, count, tiles, dense, turned, held, sems):
+def dense_kernel(core, count, ids_hbm, tiles, dense, fetched, ids, sems, ids_sem):
     mine = core[0, 0]
+    ids_copy = pltpu.make_async_copy(ids_hbm, ids, ids_sem)
+    ids_copy.start()
     copies = []
     for i in range(LOADS):
         part = pl.ds(i * LOAD, LOAD)
-        copies.append(pltpu.make_async_copy(tiles.at[part], held.at[part], sems.at[i]))
+        copies.append(pltpu.make_async_copy(tiles.at[part], fetched.at[part], sems.at[i]))
     for copy in copies:
         copy.start()
+    ids_copy.wait()
     for i in range(LOADS):
         copies[i].wait()
         for k in range(i * LOAD, (i + 1) * LOAD):
             r = ids[0, k]
             c = pl.multiple_of(ids[1, k] * TILE, TILE)
-            tile = jnp.where(k < count[0, 0], held[k], jnp.zeros((TILE, TILE), bf16))
+            tile = jnp.where(k < count[0, 0], fetched[k], jnp.zeros((TILE, TILE), bf16))
+            place = jnp.where(r < NEAR, 2 * r, 15 - 2 * r)
             for part in range(TILE // USERS):
                 half = lax.rem(part + mine, 2)
-                row = pl.multiple_of(r * (TILE // 2) + part // 2 * USERS, USERS)
+                row = pl.multiple_of((place + part // 2 * (PEERS // 2)) * USERS, USERS)
                 dense[half, pl.ds(row, USERS), pl.ds(c, TILE)] = tile[part * USERS : (part + 1) * USERS]
-            turned[pl.ds(c, TILE), pl.ds(pl.multiple_of(r * TILE, TILE), TILE)] = tile.T
 
 
 def make_dense(core, ids, count, tiles):
     return pl.pallas_call(
         dense_kernel,
-        out_shape=(
-            jax.ShapeDtypeStruct((2, HALF, BLOCK), bf16),
-            jax.ShapeDtypeStruct((BLOCK, BLOCK), bf16),
-        ),
-        in_specs=[SMEM, SMEM, SMEM, ANY],
-        out_specs=(VMEM, VMEM),
-        scratch_shapes=[pltpu.VMEM((SLOTS, TILE, TILE), bf16), pltpu.SemaphoreType.DMA((LOADS,))],
+        out_shape=jax.ShapeDtypeStruct((2, HALF, BLOCK), bf16),
+        in_specs=[SMEM, SMEM, ANY, ANY],
+        out_specs=VMEM,
+        scratch_shapes=[
+            pltpu.VMEM((SLOTS, TILE, TILE), bf16),
+            pltpu.SMEM((2, SLOTS), jnp.int32),
+            pltpu.SemaphoreType.DMA((LOADS,)),
+            pltpu.SemaphoreType.DMA,
+        ],
         compiler_params=params(),
         cost_estimate=cost(0, 3 * 2 * BLOCK * BLOCK),
         name="dense_block",
-    )(core, ids, count, held(tiles))
+    )(core, count, held(ids), held(tiles))
+
+
+def turn_kernel(dense, after, turned):
+    for half in range(2):
+        for i in range(0, HALF, TILE):
+            for j in range(0, BLOCK, TILE):
+                turned[j : j + TILE, half * HALF + i : half * HALF + i + TILE] = dense[half, i : i + TILE, j : j + TILE].T
+
+
+def turn(dense, after):
+    return pl.pallas_call(
+        turn_kernel,
+        out_shape=jax.ShapeDtypeStruct((BLOCK, BLOCK), bf16),
+        in_specs=[VMEM, ANY],
+        out_specs=VMEM,
+        compiler_params=params(),
+        cost_estimate=cost(0, 4 * BLOCK * BLOCK),
+        name="turned_block",
+    )(dense, after)
 
 
 CHUNK = 256
@@ -134,16 +160,19 @@
         out[i : i + CHUNK] = jnp.dot(dense[1, i : i + CHUNK], items[...], preferred_element_type=f32).astype(bf16)
 
 
-def mine_kernel(dense, items, other, out):
+def mine_kernel(dense, items, out):
     for i in range(0, HALF, CHUNK):
-        part = jnp.dot(dense[0, i : i + CHUNK], items[...], preferred_element_type=f32)
-        out[i : i + CHUNK] = (part + other[i : i + CHUNK].astype(f32)).astype(bf16)
-
-
-def half_product(kernel, *operands):
+        out[i : i + CHUNK] = jnp.dot(dense[0, i : i + CHUNK], items[...], preferred_element_type=f32)
+
+
+def add_kernel(mine, other, out):
+    out[...] = (mine[...] + other[...].astype(f32)).astype(bf16)
+
+
+def half_product(kernel, dtype, *operands):
     return pl.pallas_call(
         kernel,
-        out_shape=jax.ShapeDtypeStruct((HALF, 2 * WIDTH), bf16),
+        out_shape=jax.ShapeDtypeStruct((HALF, 2 * WIDTH), dtype),
         in_specs=[VMEM] * len(operands),
         out_specs=VMEM,
         compiler_params=params(),
@@ -177,7 +206,7 @@
     for i in range(PEERS):
         out[i, :USERS] = mapped
         for k in range(2):
-            rows = slice((2 * i + k) * half, (2 * i + k + 1) * half)
+            rows = slice((2 * COLS[i] + k) * half, (2 * COLS[i] + k + 1) * half)
             both = jnp.concatenate([grad_one[rows], grad_two[rows]], axis=0)
             out[i, USERS + k * GRADS : USERS + (k + 1) * GRADS] = both.astype(bf16)
 
@@ -193,34 +222,54 @@
     )(parts, w_first, w_second)
 
 
-def back_kernel(core, got, other, turned, out, mapped):
-    mine = core[0, 0]
-    slot = pl.multiple_of(USERS + mine * GRADS, GRADS)
+def own_kernel(got, turned, out, mapped):
+    for i in range(PEERS):
+        mapped[i * USERS : (i + 1) * USERS] = got[i, :USERS]
+    for i in range(0, BLOCK, CHUNK):
+        out[i : i + CHUNK] = jnp.dot(turned[i : i + CHUNK, :HALF], mapped[...], preferred_element_type=f32)
+
+
+def own_product(got, turned):
+    return pl.pallas_call(
+        own_kernel,
+        out_shape=jax.ShapeDtypeStruct((BLOCK, WIDTH), f32),
+        in_specs=[VMEM, VMEM],
+        out_specs=VMEM,
+        scratch_shapes=[pltpu.VMEM((HALF, WIDTH), bf16)],
+        compiler_params=params(),
+        cost_estimate=cost(2 * BLOCK * HALF * WIDTH, 3 * 1024 * 1024),
+        name="own_product",
+    )(got, turned)
+
+
+def back_kernel(core, got, other, own, turned, out, mapped):
+    slot = pl.multiple_of(USERS + core[0, 0] * GRADS, GRADS)
     grads = jnp.zeros((GRADS, WIDTH), f32)
     for i in range(PEERS):
         grads = grads + got[i, pl.ds(slot, GRADS)].astype(f32) + other[i, pl.ds(slot, GRADS)].astype(f32)
-        mapped[pl.ds(pl.multiple_of((2 * i + mine) * USERS, USERS), USERS)] = got[i, :USERS]
-        mapped[pl.ds(pl.multiple_of((2 * i + 1 - mine) * USERS, USERS), USERS)] = other[i, :USERS]
+        mapped[i * USERS : (i + 1) * USERS] = other[i, :USERS]
     grads = grads.astype(bf16)
     for i in range(N_ROW):
         out[i, ITEMS:] = grads
     per = CHUNK // ITEMS
     for i in range(N_ROW // per):
-        part = jnp.dot(turned[i * CHUNK : (i + 1) * CHUNK], mapped[...], preferred_element_type=f32).astype(bf16)
+        rows = slice(i * CHUNK, (i + 1) * CHUNK)
+        part = own[rows] + jnp.dot(turned[rows, HALF:], mapped[...], preferred_element_type=f32)
+        part = part.astype(bf16)
         for j in range(per):
             out[i * per + j, :ITEMS] = part[j * ITEMS : (j + 1) * ITEMS]
 
 
-def back_product(core, got, other, turned):
+def back_product(core, got, other, own, turned):
     return pl.pallas_call(
         back_kernel,
         out_shape=jax.ShapeDtypeStruct((N_ROW, ITEMS + GRADS, WIDTH), bf16),
-        in_specs=[SMEM, VMEM, VMEM, VMEM],
-        out_specs=VMEM,
-        scratch_shapes=[pltpu.VMEM((BLOCK, WIDTH), bf16)],
+        in_specs=[SMEM, VMEM, VMEM, VMEM, VMEM],
+        out_specs=VMEM,
+        scratch_shapes=[pltpu.VMEM((HALF, WIDTH), bf16)],
         compiler_params=params(),
         name="back_product",
-    )(core, got, other, turned)
+    )(core, got, other, own, turned)
 
 
 def last_kernel(got, out):
@@ -245,21 +294,25 @@
 
 def shards(features, cotangent, w_first, w_second, adjacency_tiles, tile_ids, counts):
     core = lax.rem(lax.axis_index("col"), 2).reshape(1, 1)
-    same_core = [[2 * i + k for i in range(PEERS)] for k in range(2)]
-    swap = [(i, i ^ 1) for i in range(N_COL)]
+    same_core = [[2 * i + k for i in COLS] for k in range(2)]
     same_x = [[NEAR * i + k for k in range(NEAR)] for i in range(NEAR)]
     same_z = [[NEAR * i + k for i in range(NEAR)] for k in range(NEAR)]
+    swap = [(i, i ^ 1) for i in range(N_COL)]
     spread = first_spread(features, cotangent)
-    dense, turned = make_dense(core, tile_ids[0, 0], counts, adjacency_tiles[0, 0])
+    dense = make_dense(core, tile_ids[0, 0], counts, adjacency_tiles[0, 0])
     items = lax.all_to_all(spread, "row", 0, 0, axis_index_groups=same_x).reshape(NEAR * ITEMS, 2 * WIDTH)
-    items = lax.all_to_all(second_spread(items, dense), "row", 0, 0, axis_index_groups=same_z).reshape(BLOCK, 2 * WIDTH)
-    other = lax.ppermute(half_product(theirs_kernel, dense, items), "col", swap)
-    sums = half_product(mine_kernel, dense, items, other).reshape(PEERS, USERS, 2 * WIDTH)
+    items = lax.all_to_all(second_spread(items, dense), "row", 0, 0, axis_index_groups=same_z)
+    items = items.reshape(BLOCK, 2 * WIDTH)
+    theirs = half_product(theirs_kernel, bf16, dense, items)
+    other = lax.ppermute(theirs, "col", swap)
+    mine = half_product(mine_kernel, f32, dense, items)
+    turned = turn(dense, theirs)
+    sums = half_product(add_kernel, bf16, mine, other).reshape(PEERS, USERS, 2 * WIDTH)
     parts = lax.all_to_all(sums, "col", 0, 0, axis_index_groups=same_core)
     sent = middle(parts, w_first, w_second)
     got = lax.all_to_all(sent, "col", 0, 0, axis_index_groups=same_core)
     other = lax.ppermute(got, "col", swap)
-    sent = back_product(core, got, other, turned)
+    sent = back_product(core, got, other, own_product(got, turned), turned)
     got = lax.all_to_all(sent, "row", 0, 0)
     item_out = jnp.sum(got[:, :ITEMS].astype(f32), axis=0).astype(bf16)
     grads = lax.all_to_all(last_spread(got), "col", 0, 0)

time: 141 us -> 139 us (0.986)
  blocking collectives: 83.5 us -> 80.5 us
  local copies, waits for them, and re-layouts: 2.02 us -> 0.01 us
  starting transfers between devices: 27.9 us -> 29.9 us
  waiting for transfers between devices: 16 us -> 17.7 us
    all_to_all x1, waiting for transfers between devices: 2.27 us -> 5.74 us  [shards(): lax.all_to_all(spread, 'row', 0, 0, axis_index_groups=same_x)]
    all_to_all x1, blocking collectives: 19.9 us -> 17.4 us  [shards(): got = lax.all_to_all(sent, 'col', 0, 0, axis_index_groups=same_core)]
    unnamed x10 -> x4, local copies, waits for them, and re-layouts: 2.02 us -> 0.01 us
    pallas_call x1 -> x3, Pallas kernels: 3.19 us -> 2.85 us  [the longest x1 1.74 us: make_dense(): pl.pallas_call(dense_kernel, out_shape=jax.ShapeDtypeStruct((2, HALF, BLO...]
  transfers between devices with their start and end apart: 4 -> 4, of which waited for: 4 -> 4; matrix products, arithmetic and copies ran while one was open for 0% -> 0% of each run, Pallas kernels for 2% -> 3%
where the time goes in v4:
time: 139 us
  blocking collectives  80.5 us (58%)
  starting transfers between devices  29.9 us (22%)
  waiting for transfers between devices  17.7 us (13%)
  Pallas kernels  7.75 us (6%)
  other arithmetic  1.51 us (1%)
    all_to_all x1, blocking collectives, shards(): parts = lax.all_to_all(sums, 'col', 0, 0, axis_index_groups=same_core)  25.3 us
    all_to_all x1, blocking collectives, shards(): got = lax.all_to_all(sent, 'row', 0, 0)  23.4 us
    all_to_all x1, blocking collectives, shards(): got = lax.all_to_all(sent, 'col', 0, 0, axis_index_groups=same_core)  17.4 us
    all_to_all x1, blocking collectives, shards(): lax.all_to_all(second_spread(items, dense), 'row', 0, 0, axis_index_group...  14.4 us
    all_to_all x1, starting transfers between devices, shards(): lax.all_to_all(spread, 'row', 0, 0, axis_index_groups=same_x)  10.9 us
    all_to_all x1, waiting for transfers between devices, shards(): grads = lax.all_to_all(last_spread(got), 'col', 0, 0)  10.8 us
    ppermute x1, starting transfers between devices, shards(): other = lax.ppermute(theirs, 'col', swap)  7.33 us
    all_to_all x1, starting transfers between devices, shards(): grads = lax.all_to_all(last_spread(got), 'col', 0, 0)  5.97 us
  transfers between devices with their start and end apart: 4, of which 4 were waited for; matrix products, arithmetic and copies ran while one was open for 0% of the time, Pallas kernels for 3%

profile of v4, /device:TPU:1, one launch (start us, length us, event | category | flops | bytes accessed | tf_op | source)
XLA Modules:
  0.0 138.8 jit_solution(7478615302122419164)
XLA Ops:
  0.6 1.5 %first_spread.1 = bf16[4,64,512]{2,1,0:T(8,128)(2,1)} custom-call(bf16[64,256]{1,0:T(8,128)(2,1)} %features.1, bf16[64,256]{1,0:T(8,128)(2,1)} %cotangent.1), custom_call_target="tpu_custom_call" | custom-call | bytes 524288 | tf_op jit(solution)/shard_map/first_spread/pallas_call | solution.py:58
  2.2 10.9 %all-to-all-start = ((bf16[4,64,512]{2,1,0:T(8,128)(2,1)}), bf16[4,64,512]{2,1,0:T(8,128)(2,1)S(1)}, u32[]{:S(2)}, u32[]{:S(2)}) async-start(bf16[4,64,512]{2,1,0:T(8,128)(2,1)} %first_spread.1), calls=%async_computation | async-start | bytes 524288 | tf_op jit(solution)/shard_map/all_to_all | solution.py:303
  13.7 1.7 %dense_block.1.after.dense = bf16[2,512,1024]{2,1,0:T(8,128)(2,1)S(1)} custom-call(s32[1,1]{1,0:T(1,128)} %bitcast.core, s32[1,1]{1,0:T(1,128)S(6)} %copy.10.count, s32[2,64]{1,0:T(2,128)} %bitcast.21, bf16[64,128,128]{2,1,0:T(8,128)(2,1)} %bitcast.20), custom_call_target="tpu_custom_call" | custom-call | bytes 6291456 | tf_op jit(solution)/shard_map/dense_block/pallas_call | solution.py:119
  15.4 5.7 %all-to-all-done = bf16[4,64,512]{2,1,0:T(8,128)(2,1)S(1)} async-done(((bf16[4,64,512]{2,1,0:T(8,128)(2,1)}), bf16[4,64,512]{2,1,0:T(8,128)(2,1)S(1)}, u32[]{:S(2)}, u32[]{:S(2)}) %all-to-all-start) | async-done | bytes 262176 | tf_op jit(solution)/shard_map/all_to_all | solution.py:303
  21.2 0.1 second_spread.1
  21.2 14.4 %all_to_all.30 = bf16[4,256,512]{2,1,0:T(8,128)(2,1)S(1)} all-to-all(bf16[4,256,512]{2,1,0:T(8,128)(2,1)S(1)} %second_spread.1), channel_id=1, replica_groups={{0,128,256,384},{32,160,288,416},{64,192,320,448},{96,224,352,480},{1,1..., dimensions={0} | all-to-all | bytes 2097152 | tf_op jit(solution)/shard_map/all_to_all | solution.py:304
  35.7 0.7 user_product.4.after
  36.4 7.3 %collective-permute-start = (bf16[512,512]{1,0:T(8,128)(2,1)S(1)}, bf16[512,512]{1,0:T(8,128)(2,1)S(1)}, u32[]{:S(2)}, u32[]{:S(2)}) collective-permute-start(bf16[512,512]{1,0:T(8,128)(2,1)S(1)} %user_product.4.after), channel_id=1, source_target_pairs={{0,1},{1,0},{2,3},{3,2},{4,5},{5,4},{6,7},{7,6},{8,9},{9,8},{10,11... | collective-permute-start | bytes 1572872 | tf_op jit(solution)/shard_map/ppermute | solution.py:307
  43.7 0.7 user_product.3.mine
  44.4 0.0 copy-start
  44.4 0.0 copy-start.1
  44.4 0.8 collective-permute-done.other
  45.2 0.1 user_product.5
  45.3 25.3 %all_to_all.31.parts = bf16[16,32,512]{2,1,0:T(8,128)(2,1)S(1)} all-to-all(bf16[16,32,512]{2,1,0:T(8,128)(2,1)S(1)} %bitcast.18), channel_id=1, replica_groups={{0,28,4,24,8,20,12,16,2,30,6,26,10,22,14,18},{1,29,5,25,9,21,13,17,3,31..., dimensions={0} | all-to-all | bytes 1048576 | tf_op jit(solution)/shard_map/all_to_all | solution.py:311
  70.6 0.0 copy-done
  70.6 0.0 copy-done.1
  70.6 0.6 middle.1
  71.2 17.4 %all_to_all.32.got = bf16[16,64,256]{2,1,0:T(8,128)(2,1)S(1)} all-to-all(bf16[16,64,256]{2,1,0:T(8,128)(2,1)S(1)} %middle.1), channel_id=1, replica_groups={{0,28,4,24,8,20,12,16,2,30,6,26,10,22,14,18},{1,29,5,25,9,21,13,17,3,31..., dimensions={0} | all-to-all | bytes 1048576 | tf_op jit(solution)/shard_map/all_to_all | solution.py:313
  88.7 5.7 %collective-permute-start.1 = (bf16[16,64,256]{2,1,0:T(8,128)(2,1)S(1)}, bf16[16,64,256]{2,1,0:T(8,128)(2,1)S(1)}, u32[]{:S(2)}, u32[]{:S(2)}) collective-permute-start(bf16[16,64,256]{2,1,0:T(8,128)(2,1)S(1)} %all_to_all.32.got), channel_id=1, source_target_pairs={{0,1},{1,0},{2,3},{3,2},{4,5},{5,4},{6,7},{7,6},{8,9},{9,8},{10,11... | collective-permute-start | bytes 1572872 | tf_op jit(solution)/shard_map/ppermute | solution.py:314
  94.4 0.7 turned_block.1.turned
  95.1 0.4 own_product.1.own
  95.5 0.4 collective-permute-done.1.other
  95.9 0.4 back_product.1
  96.3 23.4 %all_to_all.33.got = bf16[16,80,256]{2,1,0:T(8,128)(2,1)S(1)} all-to-all(bf16[16,80,256]{2,1,0:T(8,128)(2,1)S(1)} %back_product.1), channel_id=1, replica_groups=mesh['row'=16,'col'=32] {'row'}, dimensions={0} | all-to-all | bytes 1310720 | tf_op jit(solution)/shard_map/all_to_all | solution.py:316
  119.8 0.7 last_spread.1
  120.5 6.0 %all-to-all-start.5 = ((bf16[32,16,256]{2,1,0:T(8,128)(2,1)}), bf16[32,16,256]{2,1,0:T(8,128)(2,1)S(1)}, u32[]{:S(2)}, u32[]{:S(2)}) async-start(bf16[32,16,256]{2,1,0:T(8,128)(2,1)} %last_spread.1), calls=%async_computation.5 | async-start | bytes 524288 | tf_op jit(solution)/shard_map/all_to_all | solution.py:318
  126.5 0.7 slice_reduce_fusion
  127.2 10.8 %all-to-all-done.5 = bf16[32,16,256]{2,1,0:T(8,128)(2,1)S(1)} async-done(((bf16[32,16,256]{2,1,0:T(8,128)(2,1)}), bf16[32,16,256]{2,1,0:T(8,128)(2,1)S(1)}, u32[]{:S(2)}, u32[]{:S(2)}) %all-to-all-start.5) | async-done | bytes 262176 | tf_op jit(solution)/shard_map/all_to_all | solution.py:318
  137.9 0.8 fusion
Async XLA Ops:
  2.2 19.0 %all-to-all-start = ((bf16[4,64,512]{2,1,0:T(8,128)(2,1)}), bf16[4,64,512]{2,1,0:T(8,128)(2,1)S(1)}, u32[]{:S(2)}, u32[]{:S(2)}) async-start(bf16[4,64,512]{2,1,0:T(8,128)(2,1)} %first_spread.1), calls=%async_computation | async-start | bytes 524288 | tf_op jit(solution)/shard_map/all_to_all | solution.py:303
  36.4 8.9 %collective-permute-start = (bf16[512,512]{1,0:T(8,128)(2,1)S(1)}, bf16[512,512]{1,0:T(8,128)(2,1)S(1)}, u32[]{:S(2)}, u32[]{:S(2)}) collective-permute-start(bf16[512,512]{1,0:T(8,128)(2,1)S(1)} %user_product.4.after), channel_id=1, source_target_pairs={{0,1},{1,0},{2,3},{3,2},{4,5},{5,4},{6,7},{7,6},{8,9},{9,8},{10,11... | collective-permute-start | bytes 1572872 | tf_op jit(solution)/shard_map/ppermute | solution.py:307
  44.4 26.2 %copy-start = (bf16[256,256]{1,0:T(8,128)(2,1)S(1)}, bf16[256,256]{1,0:T(8,128)(2,1)}, u32[]{:S(2)}) copy-start(bf16[256,256]{1,0:T(8,128)(2,1)} %w_first.1) | copy-start | bytes 393220
  44.4 26.2 %copy-start.1 = (bf16[256,256]{1,0:T(8,128)(2,1)S(1)}, bf16[256,256]{1,0:T(8,128)(2,1)}, u32[]{:S(2)}) copy-start(bf16[256,256]{1,0:T(8,128)(2,1)} %w_second.1) | copy-start | bytes 393220
  88.7 7.2 %collective-permute-start.1 = (bf16[16,64,256]{2,1,0:T(8,128)(2,1)S(1)}, bf16[16,64,256]{2,1,0:T(8,128)(2,1)S(1)}, u32[]{:S(2)}, u32[]{:S(2)}) collective-permute-start(bf16[16,64,256]{2,1,0:T(8,128)(2,1)S(1)} %all_to_all.32.got), channel_id=1, source_target_pairs={{0,1},{1,0},{2,3},{3,2},{4,5},{5,4},{6,7},{7,6},{8,9},{9,8},{10,11... | collective-permute-start | bytes 1572872 | tf_op jit(solution)/shard_map/ppermute | solution.py:314
  120.5 17.4 %all-to-all-start.5 = ((bf16[32,16,256]{2,1,0:T(8,128)(2,1)}), bf16[32,16,256]{2,1,0:T(8,128)(2,1)S(1)}, u32[]{:S(2)}, u32[]{:S(2)}) async-start(bf16[32,16,256]{2,1,0:T(8,128)(2,1)} %last_spread.1), calls=%async_computation.5 | async-start | bytes 524288 | tf_op jit(solution)/shard_map/all_to_all | solution.py:318

commit v5 on v4

--- a/solution.py
+++ b/solution.py
@@ -165,7 +165,7 @@
         out[i : i + CHUNK] = jnp.dot(dense[0, i : i + CHUNK], items[...], preferred_element_type=f32)
 
 
-def add_kernel(mine, other, out):
+def add_kernel(mine, other, after, out):
     out[...] = (mine[...] + other[...].astype(f32)).astype(bf16)
 
 
@@ -173,7 +173,7 @@
     return pl.pallas_call(
         kernel,
         out_shape=jax.ShapeDtypeStruct((HALF, 2 * WIDTH), dtype),
-        in_specs=[VMEM] * len(operands),
+        in_specs=([VMEM, VMEM, ANY])[: len(operands)],
         out_specs=VMEM,
         compiler_params=params(),
         cost_estimate=cost(2 * HALF * BLOCK * 2 * WIDTH, 3 * 1024 * 1024),
@@ -181,112 +181,134 @@
     )(*operands)
 
 
-def middle_kernel(parts, w_first, w_second, out):
+def middle_kernel(parts, out):
     total = parts[0].astype(f32)
     for i in range(1, PEERS):
         total = total + parts[i].astype(f32)
-    sums = total[:, :WIDTH]
-    d_users = total[:, WIDTH:].astype(bf16)
-    high = sums.astype(bf16)
-    low = (sums - high.astype(f32)).astype(bf16)
+    total = total.astype(bf16)
+    for i in range(PEERS):
+        out[i] = total
+
+
+def middle(parts):
+    return pl.pallas_call(
+        middle_kernel,
+        out_shape=jax.ShapeDtypeStruct((PEERS, USERS, 2 * WIDTH), bf16),
+        in_specs=[VMEM],
+        out_specs=VMEM,
+        compiler_params=params(),
+        name="middle",
+    )(parts)
+
+
+def layer(core, rows, w1, w2, first, mapped):
+    sums = first[:, :WIDTH]
+    d_users = first[:, WIDTH:]
+    z = jnp.dot(sums, w1, preferred_element_type=f32)
+    s = jax.nn.sigmoid(z)
+    hidden = (z * s).astype(bf16)
+    mapped[rows] = jnp.dot(hidden, w2, preferred_element_type=f32).astype(bf16)
+    back = lax.dot_general(d_users, w2, (((1,), (1,)), ((), ())), preferred_element_type=f32)
+    d_pre = (back * s * (1.0 + z * (1.0 - s))).astype(bf16)
+    is_first = core == 0
+    left = jnp.where(is_first, sums, hidden)
+    right = jnp.where(is_first, d_pre, d_users)
+    return lax.dot_general(left, right, (((0,), (0,)), ((), ())), preferred_element_type=f32)
+
+
+def block_layer(core, got, w_first, w_second, mapped):
     w1 = w_first[...]
     w2 = w_second[...]
-    z = jnp.dot(high, w1, preferred_element_type=f32) + jnp.dot(low, w1, preferred_element_type=f32)
-    s = jax.nn.sigmoid(z)
-    hidden = (z * s).astype(bf16)
-    mapped = jnp.dot(hidden, w2, preferred_element_type=f32).astype(bf16)
-    back = lax.dot_general(d_users, w2, (((1,), (1,)), ((), ())), preferred_element_type=f32)
-    d_pre = (back * s * (1.0 + z * (1.0 - s))).astype(bf16)
-    over_users = (((0,), (0,)), ((), ()))
-    grad_one = lax.dot_general(high, d_pre, over_users, preferred_element_type=f32) + lax.dot_general(
-        low, d_pre, over_users, preferred_element_type=f32
-    )
-    grad_two = lax.dot_general(hidden, d_users, over_users, preferred_element_type=f32)
-    half = GRADS // 2
-    for i in range(PEERS):
-        out[i, :USERS] = mapped
-        for k in range(2):
-            rows = slice((2 * COLS[i] + k) * half, (2 * COLS[i] + k + 1) * half)
-            both = jnp.concatenate([grad_one[rows], grad_two[rows]], axis=0)
-            out[i, USERS + k * GRADS : USERS + (k + 1) * GRADS] = both.astype(bf16)
-
-
-def middle(parts, w_first, w_second):
-    return pl.pallas_call(
-        middle_kernel,
-        out_shape=jax.ShapeDtypeStruct((PEERS, USERS + 2 * GRADS, WIDTH), bf16),
-        in_specs=[VMEM, VMEM, VMEM],
-        out_specs=VMEM,
-        compiler_params=params(),
-        name="middle",
-    )(parts, w_first, w_second)
-
-
-def own_kernel(got, turned, out, mapped):
-    for i in range(PEERS):
-        mapped[i * USERS : (i + 1) * USERS] = got[i, :USERS]
+    grads = None
+    step = CHUNK // USERS
+    for i in range(0, PEERS, step):
+        chunk = got[i : i + step].reshape(CHUNK, 2 * WIDTH)
+        part = layer(core, slice(i * USERS, i * USERS + CHUNK), w1, w2, chunk, mapped)
+        grads = part if grads is None else grads + part
+    return grads
+
+
+def own_kernel(core, got, w_first, w_second, turned, out, grads, mapped):
+    grads[...] = block_layer(core[0, 0], got, w_first, w_second, mapped)
     for i in range(0, BLOCK, CHUNK):
         out[i : i + CHUNK] = jnp.dot(turned[i : i + CHUNK, :HALF], mapped[...], preferred_element_type=f32)
 
 
-def own_product(got, turned):
+def own_product(core, got, w_first, w_second, turned):
     return pl.pallas_call(
         own_kernel,
-        out_shape=jax.ShapeDtypeStruct((BLOCK, WIDTH), f32),
-        in_specs=[VMEM, VMEM],
-        out_specs=VMEM,
+        out_shape=(jax.ShapeDtypeStruct((BLOCK, WIDTH), f32), jax.ShapeDtypeStruct((WIDTH, WIDTH), f32)),
+        in_specs=[SMEM, VMEM, VMEM, VMEM, VMEM],
+        out_specs=(VMEM, VMEM),
         scratch_shapes=[pltpu.VMEM((HALF, WIDTH), bf16)],
         compiler_params=params(),
         cost_estimate=cost(2 * BLOCK * HALF * WIDTH, 3 * 1024 * 1024),
         name="own_product",
-    )(got, turned)
-
-
-def back_kernel(core, got, other, own, turned, out, mapped):
-    slot = pl.multiple_of(USERS + core[0, 0] * GRADS, GRADS)
-    grads = jnp.zeros((GRADS, WIDTH), f32)
-    for i in range(PEERS):
-        grads = grads + got[i, pl.ds(slot, GRADS)].astype(f32) + other[i, pl.ds(slot, GRADS)].astype(f32)
-        mapped[i * USERS : (i + 1) * USERS] = other[i, :USERS]
+    )(core, got, w_first, w_second, turned)
+
+
+def back_kernel(core, got, w_first, w_second, own, own_grads, turned, out, mapped):
+    grads = own_grads[...] + block_layer(core[0, 0], got, w_first, w_second, mapped)
     grads = grads.astype(bf16)
-    for i in range(N_ROW):
-        out[i, ITEMS:] = grads
-    per = CHUNK // ITEMS
-    for i in range(N_ROW // per):
+    for i in range(NEAR):
         rows = slice(i * CHUNK, (i + 1) * CHUNK)
         part = own[rows] + jnp.dot(turned[rows, HALF:], mapped[...], preferred_element_type=f32)
-        part = part.astype(bf16)
-        for j in range(per):
-            out[i * per + j, :ITEMS] = part[j * ITEMS : (j + 1) * ITEMS]
-
-
-def back_product(core, got, other, own, turned):
+        out[i, :CHUNK] = part.astype(bf16)
+        out[i, CHUNK:] = grads[i * ITEMS : (i + 1) * ITEMS]
+
+
+def back_product(core, got, w_first, w_second, own, own_grads, turned):
     return pl.pallas_call(
         back_kernel,
-        out_shape=jax.ShapeDtypeStruct((N_ROW, ITEMS + GRADS, WIDTH), bf16),
-        in_specs=[SMEM, VMEM, VMEM, VMEM, VMEM],
+        out_shape=jax.ShapeDtypeStruct((NEAR, CHUNK + ITEMS, WIDTH), bf16),
+        in_specs=[SMEM, VMEM, VMEM, VMEM, VMEM, VMEM, VMEM],
         out_specs=VMEM,
         scratch_shapes=[pltpu.VMEM((HALF, WIDTH), bf16)],
         compiler_params=params(),
         name="back_product",
-    )(core, got, other, own, turned)
-
-
-def last_kernel(got, out):
-    grads = got[0, ITEMS:].astype(f32)
-    for i in range(1, N_ROW):
-        grads = grads + got[i, ITEMS:].astype(f32)
-    grads = grads.astype(bf16)
-    for i in range(N_COL):
-        out[i] = grads
+    )(core, got, w_first, w_second, own, own_grads, turned)
+
+
+def sum_kernel(got, out):
+    total = got[0].astype(f32)
+    for i in range(1, NEAR):
+        total = total + got[i].astype(f32)
+    total = total.astype(bf16)
+    for i in range(NEAR):
+        out[i, :ITEMS] = total[i * ITEMS : (i + 1) * ITEMS]
+        out[i, ITEMS:] = total[CHUNK:]
+
+
+def sum_sides(got):
+    return pl.pallas_call(
+        sum_kernel,
+        out_shape=jax.ShapeDtypeStruct((NEAR, 2 * ITEMS, WIDTH), bf16),
+        in_specs=[VMEM],
+        out_specs=VMEM,
+        compiler_params=params(),
+        name="sum_sides",
+    )(got)
+
+
+def last_kernel(got, item_out, out):
+    total = got[0].astype(f32)
+    for i in range(1, NEAR):
+        total = total + got[i].astype(f32)
+    total = total.astype(bf16)
+    item_out[...] = total[:ITEMS]
+    for i in range(2 * NEAR):
+        out[i] = total[ITEMS:]
 
 
 def last_spread(got):
     return pl.pallas_call(
         last_kernel,
-        out_shape=jax.ShapeDtypeStruct((N_COL, GRADS, WIDTH), bf16),
+        out_shape=(
+            jax.ShapeDtypeStruct((ITEMS, WIDTH), bf16),
+            jax.ShapeDtypeStruct((2 * NEAR, ITEMS, WIDTH), bf16),
+        ),
         in_specs=[VMEM],
-        out_specs=VMEM,
+        out_specs=(VMEM, VMEM),
         compiler_params=params(),
         name="last_spread",
     )(got)
@@ -297,6 +319,11 @@
     same_core = [[2 * i + k for i in COLS] for k in range(2)]
     same_x = [[NEAR * i + k for k in range(NEAR)] for i in range(NEAR)]
     same_z = [[NEAR * i + k for i in range(NEAR)] for k in range(NEAR)]
+    sides = [
+        [(NEAR * i + k) * N_COL + 2 * q + h for h in range(2) for i in range(NEAR)]
+        for k in range(NEAR)
+        for q in range(PEERS)
+    ]
     swap = [(i, i ^ 1) for i in range(N_COL)]
     spread = first_spread(features, cotangent)
     dense = make_dense(core, tile_ids[0, 0], counts, adjacency_tiles[0, 0])
@@ -307,18 +334,17 @@
     other = lax.ppermute(theirs, "col", swap)
     mine = half_product(mine_kernel, f32, dense, items)
     turned = turn(dense, theirs)
-    sums = half_product(add_kernel, bf16, mine, other).reshape(PEERS, USERS, 2 * WIDTH)
+    sums = half_product(add_kernel, bf16, mine, other, turned).reshape(PEERS, USERS, 2 * WIDTH)
     parts = lax.all_to_all(sums, "col", 0, 0, axis_index_groups=same_core)
-    sent = middle(parts, w_first, w_second)
-    got = lax.all_to_all(sent, "col", 0, 0, axis_index_groups=same_core)
+    got = lax.all_to_all(middle(parts), "col", 0, 0, axis_index_groups=same_core)
     other = lax.ppermute(got, "col", swap)
-    sent = back_product(core, got, other, own_product(got, turned), turned)
-    got = lax.all_to_all(sent, "row", 0, 0)
-    item_out = jnp.sum(got[:, :ITEMS].astype(f32), axis=0).astype(bf16)
-    grads = lax.all_to_all(last_spread(got), "col", 0, 0)
-    half = GRADS // 2
-    grad_one = grads[:, :half].astype(f32).reshape(WIDTH, WIDTH)
-    grad_two = grads[:, half:].astype(f32).reshape(WIDTH, WIDTH)
+    own, own_grads = own_product(core, got, w_first, w_second, turned)
+    sent = back_product(core, other, w_first, w_second, own, own_grads, turned)
+    sent = sum_sides(lax.all_to_all(sent, "row", 0, 0, axis_index_groups=same_z))
+    item_out, grads = last_spread(lax.all_to_all(sent, "row", 0, 0, axis_index_groups=same_x))
+    grads = lax.all_to_all(grads, ("row", "col"), 0, 0, axis_index_groups=sides).astype(f32)
+    grad_one = grads[:NEAR].reshape(WIDTH, WIDTH)
+    grad_two = grads[NEAR:].reshape(WIDTH, WIDTH)
     return (item_out, grad_one, grad_two)
 
 

time: 139 us -> 135 us (0.971)
  blocking collectives: 80.5 us -> 93.6 us
  waiting for transfers between devices: 17.7 us -> 6.25 us
  starting transfers between devices: 29.9 us -> 23.9 us
  other arithmetic: 1.51 us -> 0 us
    all_to_all x2 -> x4, blocking collectives: 40.8 us -> 53.7 us  [the longest x1 17.4 us: shards(): lax.all_to_all(middle(parts), 'col', 0, 0, axis_index_groups=same_core)]
    all_to_all x1 -> x0, waiting for transfers between devices: 10.8 us -> none  [shards(): grads = lax.all_to_all(last_spread(got), 'col', 0, 0)]
    all_to_all x1 -> x0, starting transfers between devices: 5.97 us -> none  [shards(): grads = lax.all_to_all(last_spread(got), 'col', 0, 0)]
    pallas_call x3 -> x4, Pallas kernels: 1.61 us -> 2.91 us  [the longest x1 1.1 us: back_product(): pl.pallas_call(back_kernel, out_shape=jax.ShapeDtypeStruct((NEAR, CHUNK +...]
  transfers between devices with their start and end apart: 4 -> 3, of which waited for: 4 -> 3; matrix products, arithmetic and copies ran while one was open for 0% -> 0% of each run, Pallas kernels for 3% -> 3%
where the time goes in v5:
time: 135 us; the launch traced here: 134 us
  blocking collectives  93.6 us (69%)
  starting transfers between devices  23.9 us (18%)
  Pallas kernels  8.49 us (6%)
  waiting for transfers between devices  6.25 us (5%)
  between operations  1.41 us (1%)
    all_to_all x1, blocking collectives, shards(): parts = lax.all_to_all(sums, 'col', 0, 0, axis_index_groups=same_core)  25.4 us
    all_to_all x1, blocking collectives, shards(): lax.all_to_all(middle(parts), 'col', 0, 0, axis_index_groups=same_core)  17.4 us
    all_to_all x1, blocking collectives, shards(): lax.all_to_all(second_spread(items, dense), 'row', 0, 0, axis_index_group...  14.4 us
    all_to_all x1, blocking collectives, shards(): lax.all_to_all(sent, 'row', 0, 0, axis_index_groups=same_z)  13 us
    all_to_all x1, blocking collectives, shards(): lax.all_to_all(grads, ('row', 'col'), 0, 0, axis_index_groups=sides)  12.5 us
    all_to_all x1, starting transfers between devices, shards(): lax.all_to_all(spread, 'row', 0, 0, axis_index_groups=same_x)  10.9 us
    all_to_all x1, blocking collectives, shards(): lax.all_to_all(sent, 'row', 0, 0, axis_index_groups=same_x)  10.8 us
    ppermute x1, starting transfers between devices, shards(): other = lax.ppermute(theirs, 'col', swap)  7.33 us
  transfers between devices with their start and end apart: 3, of which 3 were waited for; matrix products, arithmetic and copies ran while one was open for 0% of the time, Pallas kernels for 3%

profile of v5, /device:TPU:1, one launch (start us, length us, event | category | flops | bytes accessed | tf_op | source)
XLA Modules:
  0.0 134.5 jit_solution(14355989849378133380)
XLA Ops:
  0.6 1.5 %first_spread.1 = bf16[4,64,512]{2,1,0:T(8,128)(2,1)} custom-call(bf16[64,256]{1,0:T(8,128)(2,1)} %features.1, bf16[64,256]{1,0:T(8,128)(2,1)} %cotangent.1), custom_call_target="tpu_custom_call" | custom-call | bytes 524288 | tf_op jit(solution)/shard_map/first_spread/pallas_call | solution.py:58
  2.2 10.9 %all-to-all-start = ((bf16[4,64,512]{2,1,0:T(8,128)(2,1)}), bf16[4,64,512]{2,1,0:T(8,128)(2,1)S(1)}, u32[]{:S(2)}, u32[]{:S(2)}) async-start(bf16[4,64,512]{2,1,0:T(8,128)(2,1)} %first_spread.1), calls=%async_computation | async-start | bytes 524288 | tf_op jit(solution)/shard_map/all_to_all | solution.py:330
  13.7 1.7 %dense_block.1.after.dense = bf16[2,512,1024]{2,1,0:T(8,128)(2,1)S(1)} custom-call(s32[1,1]{1,0:T(1,128)} %bitcast.core, s32[1,1]{1,0:T(1,128)S(6)} %copy.10.count, s32[2,64]{1,0:T(2,128)} %bitcast.15, bf16[64,128,128]{2,1,0:T(8,128)(2,1)} %bitcast.12), custom_call_target="tpu_custom_call" | custom-call | bytes 6291456 | tf_op jit(solution)/shard_map/dense_block/pallas_call | solution.py:119
  15.4 5.7 %all-to-all-done = bf16[4,64,512]{2,1,0:T(8,128)(2,1)S(1)} async-done(((bf16[4,64,512]{2,1,0:T(8,128)(2,1)}), bf16[4,64,512]{2,1,0:T(8,128)(2,1)S(1)}, u32[]{:S(2)}, u32[]{:S(2)}) %all-to-all-start) | async-done | bytes 262176 | tf_op jit(solution)/shard_map/all_to_all | solution.py:330
  21.2 0.1 second_spread.1
  21.2 14.4 %all_to_all.35 = bf16[4,256,512]{2,1,0:T(8,128)(2,1)S(1)} all-to-all(bf16[4,256,512]{2,1,0:T(8,128)(2,1)S(1)} %second_spread.1), channel_id=1, replica_groups={{0,128,256,384},{32,160,288,416},{64,192,320,448},{96,224,352,480},{1,1..., dimensions={0} | all-to-all | bytes 2097152 | tf_op jit(solution)/shard_map/all_to_all | solution.py:331
  35.7 0.7 user_product.4.after
  36.4 7.3 %collective-permute-start = (bf16[512,512]{1,0:T(8,128)(2,1)S(1)}, bf16[512,512]{1,0:T(8,128)(2,1)S(1)}, u32[]{:S(2)}, u32[]{:S(2)}) collective-permute-start(bf16[512,512]{1,0:T(8,128)(2,1)S(1)} %user_product.4.after), channel_id=1, source_target_pairs={{0,1},{1,0},{2,3},{3,2},{4,5},{5,4},{6,7},{7,6},{8,9},{9,8},{10,11... | collective-permute-start | bytes 1572872 | tf_op jit(solution)/shard_map/ppermute | solution.py:334
  43.7 0.7 turned_block.1.after.turned
  44.4 0.7 user_product.3.mine
  45.1 0.1 collective-permute-done.other
  45.2 0.1 user_product.5
  45.3 0.0 copy-start
  45.3 0.0 copy-start.1
  45.3 25.4 %all_to_all.36.parts = bf16[16,32,512]{2,1,0:T(8,128)(2,1)S(1)} all-to-all(bf16[16,32,512]{2,1,0:T(8,128)(2,1)S(1)} %bitcast.10), channel_id=1, replica_groups={{0,28,4,24,8,20,12,16,2,30,6,26,10,22,14,18},{1,29,5,25,9,21,13,17,3,31..., dimensions={0} | all-to-all | bytes 1048576 | tf_op jit(solution)/shard_map/all_to_all | solution.py:338
  70.7 0.1 middle.1
  70.8 17.4 %all_to_all.37.got = bf16[16,32,512]{2,1,0:T(8,128)(2,1)S(1)} all-to-all(bf16[16,32,512]{2,1,0:T(8,128)(2,1)S(1)} %middle.1), channel_id=1, replica_groups={{0,28,4,24,8,20,12,16,2,30,6,26,10,22,14,18},{1,29,5,25,9,21,13,17,3,31..., dimensions={0} | all-to-all | bytes 1048576 | tf_op jit(solution)/shard_map/all_to_all | solution.py:339
  88.3 5.7 %collective-permute-start.1 = (bf16[16,32,512]{2,1,0:T(8,128)(2,1)S(1)}, bf16[16,32,512]{2,1,0:T(8,128)(2,1)S(1)}, u32[]{:S(2)}, u32[]{:S(2)}) collective-permute-start(bf16[16,32,512]{2,1,0:T(8,128)(2,1)S(1)} %all_to_all.37.got), channel_id=1, source_target_pairs={{0,1},{1,0},{2,3},{3,2},{4,5},{5,4},{6,7},{7,6},{8,9},{9,8},{10,11... | collective-permute-start | bytes 1572872 | tf_op jit(solution)/shard_map/ppermute | solution.py:340
  94.0 0.0 copy-done
  94.0 0.0 copy-done.1
  94.0 1.1 own_product.1
  95.1 0.4 collective-permute-done.1.got
  95.5 1.1 back_product.1
  96.6 13.0 %all_to_all.38.got = bf16[4,320,256]{2,1,0:T(8,128)(2,1)S(1)} all-to-all(bf16[4,320,256]{2,1,0:T(8,128)(2,1)S(1)} %back_product.1), channel_id=1, replica_groups={{0,128,256,384},{32,160,288,416},{64,192,320,448},{96,224,352,480},{1,1..., dimensions={0} | all-to-all | bytes 1310720 | tf_op jit(solution)/shard_map/all_to_all | solution.py:343
  109.6 0.1 sum_sides.1
  109.7 10.8 %all_to_all.39.got = bf16[4,128,256]{2,1,0:T(8,128)(2,1)S(1)} all-to-all(bf16[4,128,256]{2,1,0:T(8,128)(2,1)S(1)} %sum_sides.1), channel_id=1, replica_groups={{0,32,64,96},{128,160,192,224},{256,288,320,352},{384,416,448,480},{1,3..., dimensions={0} | all-to-all | bytes 524288 | tf_op jit(solution)/shard_map/all_to_all | solution.py:344
  120.5 0.6 last_spread.1
  121.1 12.5 %all_to_all.40 = bf16[8,64,256]{2,1,0:T(8,128)(2,1)S(1)} all-to-all(bf16[8,64,256]{2,1,0:T(8,128)(2,1)S(1)} %get-tuple-element.10), channel_id=1, replica_groups={{0,128,256,384,1,129,257,385},{2,130,258,386,3,131,259,387},{4,132,260,..., dimensions={0} | all-to-all | bytes 524288 | tf_op jit(solution)/shard_map/all_to_all | solution.py:345
  133.6 0.8 fusion
Async XLA Ops:
  2.2 19.0 %all-to-all-start = ((bf16[4,64,512]{2,1,0:T(8,128)(2,1)}), bf16[4,64,512]{2,1,0:T(8,128)(2,1)S(1)}, u32[]{:S(2)}, u32[]{:S(2)}) async-start(bf16[4,64,512]{2,1,0:T(8,128)(2,1)} %first_spread.1), calls=%async_computation | async-start | bytes 524288 | tf_op jit(solution)/shard_map/all_to_all | solution.py:330
  36.4 8.9 %collective-permute-start = (bf16[512,512]{1,0:T(8,128)(2,1)S(1)}, bf16[512,512]{1,0:T(8,128)(2,1)S(1)}, u32[]{:S(2)}, u32[]{:S(2)}) collective-permute-start(bf16[512,512]{1,0:T(8,128)(2,1)S(1)} %user_product.4.after), channel_id=1, source_target_pairs={{0,1},{1,0},{2,3},{3,2},{4,5},{5,4},{6,7},{7,6},{8,9},{9,8},{10,11... | collective-permute-start | bytes 1572872 | tf_op jit(solution)/shard_map/ppermute | solution.py:334
  45.3 48.7 %copy-start = (bf16[256,256]{1,0:T(8,128)(2,1)S(1)}, bf16[256,256]{1,0:T(8,128)(2,1)}, u32[]{:S(2)}) copy-start(bf16[256,256]{1,0:T(8,128)(2,1)} %w_first.3) | copy-start | bytes 393220
  45.3 48.7 %copy-start.1 = (bf16[256,256]{1,0:T(8,128)(2,1)S(1)}, bf16[256,256]{1,0:T(8,128)(2,1)}, u32[]{:S(2)}) copy-start(bf16[256,256]{1,0:T(8,128)(2,1)} %w_second.3) | copy-start | bytes 393220
  88.3 7.2 %collective-permute-start.1 = (bf16[16,32,512]{2,1,0:T(8,128)(2,1)S(1)}, bf16[16,32,512]{2,1,0:T(8,128)(2,1)S(1)}, u32[]{:S(2)}, u32[]{:S(2)}) collective-permute-start(bf16[16,32,512]{2,1,0:T(8,128)(2,1)S(1)} %all_to_all.37.got), channel_id=1, source_target_pairs={{0,1},{1,0},{2,3},{3,2},{4,5},{5,4},{6,7},{7,6},{8,9},{9,8},{10,11... | collective-permute-start | bytes 1572872 | tf_op jit(solution)/shard_map/ppermute | solution.py:340

commit v6 on v5

--- a/solution.py
+++ b/solution.py
@@ -16,6 +16,7 @@
 GRADS = 2 * WIDTH // N_COL
 PEERS = N_COL // 2
 NEAR = 4
+SIDES = (0, 2, 1, 3)
 RING = (0, 7, 1, 6, 2, 5, 3, 4)
 COLS = tuple(2 * y + half for half in range(2) for y in RING)
 HALF = BLOCK // 2
@@ -106,7 +107,9 @@
         copies[i].wait()
         for k in range(i * LOAD, (i + 1) * LOAD):
             r = ids[0, k]
-            c = pl.multiple_of(ids[1, k] * TILE, TILE)
+            c = ids[1, k]
+            side = lax.rem(c // 2, 2) * 2 + c // 4
+            c = pl.multiple_of((2 * side + lax.rem(c, 2)) * TILE, TILE)
             tile = jnp.where(k < count[0, 0], fetched[k], jnp.zeros((TILE, TILE), bf16))
             place = jnp.where(r < NEAR, 2 * r, 15 - 2 * r)
             for part in range(TILE // USERS):
@@ -254,7 +257,7 @@
         rows = slice(i * CHUNK, (i + 1) * CHUNK)
         part = own[rows] + jnp.dot(turned[rows, HALF:], mapped[...], preferred_element_type=f32)
         out[i, :CHUNK] = part.astype(bf16)
-        out[i, CHUNK:] = grads[i * ITEMS : (i + 1) * ITEMS]
+        out[i, CHUNK:] = grads[SIDES[i] * ITEMS : (SIDES[i] + 1) * ITEMS]
 
 
 def back_product(core, got, w_first, w_second, own, own_grads, turned):
@@ -290,35 +293,67 @@
     )(got)
 
 
-def last_kernel(got, item_out, out):
-    total = got[0].astype(f32)
+def spread_kernel(got, out):
+    total = got[0, ITEMS:].astype(f32)
     for i in range(1, NEAR):
-        total = total + got[i].astype(f32)
+        total = total + got[i, ITEMS:].astype(f32)
     total = total.astype(bf16)
-    item_out[...] = total[:ITEMS]
     for i in range(2 * NEAR):
-        out[i] = total[ITEMS:]
+        out[i] = total
 
 
 def last_spread(got):
     return pl.pallas_call(
-        last_kernel,
-        out_shape=(
-            jax.ShapeDtypeStruct((ITEMS, WIDTH), bf16),
-            jax.ShapeDtypeStruct((2 * NEAR, ITEMS, WIDTH), bf16),
-        ),
+        spread_kernel,
+        out_shape=jax.ShapeDtypeStruct((2 * NEAR, ITEMS, WIDTH), bf16),
         in_specs=[VMEM],
-        out_specs=(VMEM, VMEM),
+        out_specs=VMEM,
         compiler_params=params(),
         name="last_spread",
     )(got)
+
+
+def finish_kernel(got, grads, item_out, grad_one, grad_two, items, both, sems):
+    copies = [
+        pltpu.make_async_copy(items, item_out, sems.at[0]),
+        pltpu.make_async_copy(both.at[0], grad_one, sems.at[1]),
+        pltpu.make_async_copy(both.at[1], grad_two, sems.at[2]),
+    ]
+    for half in range(2):
+        for i in range(NEAR):
+            both[half, i * ITEMS : (i + 1) * ITEMS] = grads[half * NEAR + i].astype(f32)
+        copies[1 + half].start()
+    total = got[0, :ITEMS].astype(f32)
+    for i in range(1, NEAR):
+        total = total + got[i, :ITEMS].astype(f32)
+    items[...] = total.astype(bf16)
+    copies[0].start()
+    for copy in copies:
+        copy.wait()
+
+
+def finish(got, grads):
+    square = jax.ShapeDtypeStruct((WIDTH, WIDTH), f32)
+    return pl.pallas_call(
+        finish_kernel,
+        out_shape=(jax.ShapeDtypeStruct((ITEMS, WIDTH), bf16), square, square),
+        in_specs=[VMEM, VMEM],
+        out_specs=(ANY, ANY, ANY),
+        scratch_shapes=[
+            pltpu.VMEM((ITEMS, WIDTH), bf16),
+            pltpu.VMEM((2, WIDTH, WIDTH), f32),
+            pltpu.SemaphoreType.DMA((3,)),
+        ],
+        compiler_params=params(),
+        name="finish",
+    )(got, grads)
 
 
 def shards(features, cotangent, w_first, w_second, adjacency_tiles, tile_ids, counts):
     core = lax.rem(lax.axis_index("col"), 2).reshape(1, 1)
     same_core = [[2 * i + k for i in COLS] for k in range(2)]
     same_x = [[NEAR * i + k for k in range(NEAR)] for i in range(NEAR)]
-    same_z = [[NEAR * i + k for i in range(NEAR)] for k in range(NEAR)]
+    same_z = [[NEAR * i + k for i in SIDES] for k in range(NEAR)]
     sides = [
         [(NEAR * i + k) * N_COL + 2 * q + h for h in range(2) for i in range(NEAR)]
         for k in range(NEAR)
@@ -341,11 +376,9 @@
     own, own_grads = own_product(core, got, w_first, w_second, turned)
     sent = back_product(core, other, w_first, w_second, own, own_grads, turned)
     sent = sum_sides(lax.all_to_all(sent, "row", 0, 0, axis_index_groups=same_z))
-    item_out, grads = last_spread(lax.all_to_all(sent, "row", 0, 0, axis_index_groups=same_x))
-    grads = lax.all_to_all(grads, ("row", "col"), 0, 0, axis_index_groups=sides).astype(f32)
-    grad_one = grads[:NEAR].reshape(WIDTH, WIDTH)
-    grad_two = grads[NEAR:].reshape(WIDTH, WIDTH)
-    return (item_out, grad_one, grad_two)
+    got = lax.all_to_all(sent, "row", 0, 0, axis_index_groups=same_x)
+    grads = lax.all_to_all(last_spread(got), ("row", "col"), 0, 0, axis_index_groups=sides)
+    return finish(got, grads)
 
 
 def solution(mesh):

time: 135 us -> 134 us (level)
  transfers between devices with their start and end apart: 3 -> 3, of which waited for: 3 -> 3; matrix products, arithmetic and copies ran while one was open for 0% -> 0% of each run, Pallas kernels for 3% -> 4%
where the time goes in v6:
time: 134 us; the launch traced here: 133 us
  blocking collectives  93.1 us (69%)
  starting transfers between devices  23.8 us (18%)
  Pallas kernels  9.2 us (7%)
  waiting for transfers between devices  5.77 us (4%)
  between operations  1.41 us (1%)
    all_to_all x1, blocking collectives, shards(): parts = lax.all_to_all(sums, 'col', 0, 0, axis_index_groups=same_core)  25.4 us
    all_to_all x1, blocking collectives, shards(): lax.all_to_all(middle(parts), 'col', 0, 0, axis_index_groups=same_core)  17.4 us
    all_to_all x1, blocking collectives, shards(): lax.all_to_all(second_spread(items, dense), 'row', 0, 0, axis_index_group...  14.2 us
    all_to_all x1, blocking collectives, shards(): lax.all_to_all(last_spread(got), ('row', 'col'), 0, 0, axis_index_groups=...  12.7 us
    all_to_all x1, blocking collectives, shards(): lax.all_to_all(sent, 'row', 0, 0, axis_index_groups=same_z)  12.5 us
    all_to_all x1, starting transfers between devices, shards(): lax.all_to_all(spread, 'row', 0, 0, axis_index_groups=same_x)  10.9 us
    all_to_all x1, blocking collectives, shards(): got = lax.all_to_all(sent, 'row', 0, 0, axis_index_groups=same_x)  10.9 us
    ppermute x1, starting transfers between devices, shards(): other = lax.ppermute(theirs, 'col', swap)  7.25 us
  transfers between devices with their start and end apart: 3, of which 3 were waited for; matrix products, arithmetic and copies ran while one was open for 0% of the time, Pallas kernels for 4%

profile of v6, /device:TPU:1, one launch (start us, length us, event | category | flops | bytes accessed | tf_op | source)
XLA Modules:
  0.0 133.3 jit_solution(3688625419488480825)
XLA Ops:
  0.6 1.5 %first_spread.1 = bf16[4,64,512]{2,1,0:T(8,128)(2,1)} custom-call(bf16[64,256]{1,0:T(8,128)(2,1)} %features.1, bf16[64,256]{1,0:T(8,128)(2,1)} %cotangent.1), custom_call_target="tpu_custom_call" | custom-call | bytes 524288 | tf_op jit(solution)/shard_map/first_spread/pallas_call | solution.py:59
  2.2 10.9 %all-to-all-start = ((bf16[4,64,512]{2,1,0:T(8,128)(2,1)}), bf16[4,64,512]{2,1,0:T(8,128)(2,1)S(1)}, u32[]{:S(2)}, u32[]{:S(2)}) async-start(bf16[4,64,512]{2,1,0:T(8,128)(2,1)} %first_spread.1), calls=%async_computation | async-start | bytes 524288 | tf_op jit(solution)/shard_map/all_to_all | solution.py:365
  13.7 2.2 %dense_block.1.after.dense = bf16[2,512,1024]{2,1,0:T(8,128)(2,1)S(1)} custom-call(s32[1,1]{1,0:T(1,128)} %bitcast.core, s32[1,1]{1,0:T(1,128)S(6)} %copy.10.count, s32[2,64]{1,0:T(2,128)} %bitcast.11, bf16[64,128,128]{2,1,0:T(8,128)(2,1)} %bitcast.10), custom_call_target="tpu_custom_call" | custom-call | bytes 6291456 | tf_op jit(solution)/shard_map/dense_block/pallas_call | solution.py:122
  15.9 5.3 %all-to-all-done = bf16[4,64,512]{2,1,0:T(8,128)(2,1)S(1)} async-done(((bf16[4,64,512]{2,1,0:T(8,128)(2,1)}), bf16[4,64,512]{2,1,0:T(8,128)(2,1)S(1)}, u32[]{:S(2)}, u32[]{:S(2)}) %all-to-all-start) | async-done | bytes 262176 | tf_op jit(solution)/shard_map/all_to_all | solution.py:365
  21.2 0.1 second_spread.1
  21.2 14.2 %all_to_all.35 = bf16[4,256,512]{2,1,0:T(8,128)(2,1)S(1)} all-to-all(bf16[4,256,512]{2,1,0:T(8,128)(2,1)S(1)} %second_spread.1), channel_id=1, replica_groups={{0,256,128,384},{32,288,160,416},{64,320,192,448},{96,352,224,480},{1,2..., dimensions={0} | all-to-all | bytes 2097152 | tf_op jit(solution)/shard_map/all_to_all | solution.py:366
  35.5 0.7 user_product.4.after
  36.2 7.3 %collective-permute-start = (bf16[512,512]{1,0:T(8,128)(2,1)S(1)}, bf16[512,512]{1,0:T(8,128)(2,1)S(1)}, u32[]{:S(2)}, u32[]{:S(2)}) collective-permute-start(bf16[512,512]{1,0:T(8,128)(2,1)S(1)} %user_product.4.after), channel_id=1, source_target_pairs={{0,1},{1,0},{2,3},{3,2},{4,5},{5,4},{6,7},{7,6},{8,9},{9,8},{10,11... | collective-permute-start | bytes 1572872 | tf_op jit(solution)/shard_map/ppermute | solution.py:369
  43.4 0.7 turned_block.1.after.turned
  44.1 0.7 user_product.3.mine
  44.8 0.1 collective-permute-done.other
  44.9 0.1 user_product.5
  45.0 0.0 copy-start
  45.0 0.0 copy-start.1
  45.1 25.4 %all_to_all.36.parts = bf16[16,32,512]{2,1,0:T(8,128)(2,1)S(1)} all-to-all(bf16[16,32,512]{2,1,0:T(8,128)(2,1)S(1)} %bitcast.8), channel_id=1, replica_groups={{0,28,4,24,8,20,12,16,2,30,6,26,10,22,14,18},{1,29,5,25,9,21,13,17,3,31..., dimensions={0} | all-to-all | bytes 1048576 | tf_op jit(solution)/shard_map/all_to_all | solution.py:373
  70.5 0.1 middle.1
  70.5 17.4 %all_to_all.37.got = bf16[16,32,512]{2,1,0:T(8,128)(2,1)S(1)} all-to-all(bf16[16,32,512]{2,1,0:T(8,128)(2,1)S(1)} %middle.1), channel_id=1, replica_groups={{0,28,4,24,8,20,12,16,2,30,6,26,10,22,14,18},{1,29,5,25,9,21,13,17,3,31..., dimensions={0} | all-to-all | bytes 1048576 | tf_op jit(solution)/shard_map/all_to_all | solution.py:374
  88.0 5.7 %collective-permute-start.1 = (bf16[16,32,512]{2,1,0:T(8,128)(2,1)S(1)}, bf16[16,32,512]{2,1,0:T(8,128)(2,1)S(1)}, u32[]{:S(2)}, u32[]{:S(2)}) collective-permute-start(bf16[16,32,512]{2,1,0:T(8,128)(2,1)S(1)} %all_to_all.37.got), channel_id=1, source_target_pairs={{0,1},{1,0},{2,3},{3,2},{4,5},{5,4},{6,7},{7,6},{8,9},{9,8},{10,11... | collective-permute-start | bytes 1572872 | tf_op jit(solution)/shard_map/ppermute | solution.py:375
  93.7 0.0 copy-done
  93.7 0.0 copy-done.1
  93.7 1.1 own_product.1
  94.8 0.4 collective-permute-done.1.got
  95.2 1.1 back_product.1
  96.3 12.5 %all_to_all.38.got = bf16[4,320,256]{2,1,0:T(8,128)(2,1)S(1)} all-to-all(bf16[4,320,256]{2,1,0:T(8,128)(2,1)S(1)} %back_product.1), channel_id=1, replica_groups={{0,256,128,384},{32,288,160,416},{64,320,192,448},{96,352,224,480},{1,2..., dimensions={0} | all-to-all | bytes 1310720 | tf_op jit(solution)/shard_map/all_to_all | solution.py:378
  108.8 0.1 sum_sides.1
  108.9 10.9 %all_to_all.39.got = bf16[4,128,256]{2,1,0:T(8,128)(2,1)S(1)} all-to-all(bf16[4,128,256]{2,1,0:T(8,128)(2,1)S(1)} %sum_sides.1), channel_id=1, replica_groups={{0,32,64,96},{128,160,192,224},{256,288,320,352},{384,416,448,480},{1,3..., dimensions={0} | all-to-all | bytes 524288 | tf_op jit(solution)/shard_map/all_to_all | solution.py:379
  119.8 12.7 %all_to_all.40.grads = bf16[8,64,256]{2,1,0:T(8,128)(2,1)S(1)} all-to-all(bf16[8,64,256]{2,1,0:T(8,128)(2,1)S(1)} %last_spread.1), channel_id=1, replica_groups={{0,128,256,384,1,129,257,385},{2,130,258,386,3,131,259,387},{4,132,260,..., dimensions={0} | all-to-all | bytes 524288 | tf_op jit(solution)/shard_map/all_to_all | solution.py:380
  132.4 0.8 finish.1
  (1 shorter events, 0.0 us)
Async XLA Ops:
  2.2 19.0 %all-to-all-start = ((bf16[4,64,512]{2,1,0:T(8,128)(2,1)}), bf16[4,64,512]{2,1,0:T(8,128)(2,1)S(1)}, u32[]{:S(2)}, u32[]{:S(2)}) async-start(bf16[4,64,512]{2,1,0:T(8,128)(2,1)} %first_spread.1), calls=%async_computation | async-start | bytes 524288 | tf_op jit(solution)/shard_map/all_to_all | solution.py:365
  36.2 8.8 %collective-permute-start = (bf16[512,512]{1,0:T(8,128)(2,1)S(1)}, bf16[512,512]{1,0:T(8,128)(2,1)S(1)}, u32[]{:S(2)}, u32[]{:S(2)}) collective-permute-start(bf16[512,512]{1,0:T(8,128)(2,1)S(1)} %user_product.4.after), channel_id=1, source_target_pairs={{0,1},{1,0},{2,3},{3,2},{4,5},{5,4},{6,7},{7,6},{8,9},{9,8},{10,11... | collective-permute-start | bytes 1572872 | tf_op jit(solution)/shard_map/ppermute | solution.py:369
  45.0 48.7 %copy-start = (bf16[256,256]{1,0:T(8,128)(2,1)S(1)}, bf16[256,256]{1,0:T(8,128)(2,1)}, u32[]{:S(2)}) copy-start(bf16[256,256]{1,0:T(8,128)(2,1)} %w_first.3) | copy-start | bytes 393220
  45.0 48.7 %copy-start.1 = (bf16[256,256]{1,0:T(8,128)(2,1)S(1)}, bf16[256,256]{1,0:T(8,128)(2,1)}, u32[]{:S(2)}) copy-start(bf16[256,256]{1,0:T(8,128)(2,1)} %w_second.3) | copy-start | bytes 393220
  88.0 7.2 %collective-permute-start.1 = (bf16[16,32,512]{2,1,0:T(8,128)(2,1)S(1)}, bf16[16,32,512]{2,1,0:T(8,128)(2,1)S(1)}, u32[]{:S(2)}, u32[]{:S(2)}) collective-permute-start(bf16[16,32,512]{2,1,0:T(8,128)(2,1)S(1)} %all_to_all.37.got), channel_id=1, source_target_pairs={{0,1},{1,0},{2,3},{3,2},{4,5},{5,4},{6,7},{7,6},{8,9},{9,8},{10,11... | collective-permute-start | bytes 1572872 | tf_op jit(solution)/shard_map/ppermute | solution.py:375

commit v7 on v6

--- a/solution.py
+++ b/solution.py
@@ -204,72 +204,80 @@
     )(parts)
 
 
-def layer(core, rows, w1, w2, first, mapped):
-    sums = first[:, :WIDTH]
-    d_users = first[:, WIDTH:]
-    z = jnp.dot(sums, w1, preferred_element_type=f32)
-    s = jax.nn.sigmoid(z)
-    hidden = (z * s).astype(bf16)
-    mapped[rows] = jnp.dot(hidden, w2, preferred_element_type=f32).astype(bf16)
-    back = lax.dot_general(d_users, w2, (((1,), (1,)), ((), ())), preferred_element_type=f32)
-    d_pre = (back * s * (1.0 + z * (1.0 - s))).astype(bf16)
-    is_first = core == 0
-    left = jnp.where(is_first, sums, hidden)
-    right = jnp.where(is_first, d_pre, d_users)
-    return lax.dot_general(left, right, (((0,), (0,)), ((), ())), preferred_element_type=f32)
-
-
-def block_layer(core, got, w_first, w_second, mapped):
+def layer_kernel(core, got, w_first, w_second, sent, kept):
     w1 = w_first[...]
     w2 = w_second[...]
-    grads = None
+    over_users = (((0,), (0,)), ((), ()))
+    grad_one = jnp.zeros((WIDTH, WIDTH), f32)
+    grad_two = jnp.zeros((WIDTH, WIDTH), f32)
     step = CHUNK // USERS
     for i in range(0, PEERS, step):
         chunk = got[i : i + step].reshape(CHUNK, 2 * WIDTH)
-        part = layer(core, slice(i * USERS, i * USERS + CHUNK), w1, w2, chunk, mapped)
-        grads = part if grads is None else grads + part
-    return grads
-
-
-def own_kernel(core, got, w_first, w_second, turned, out, grads, mapped):
-    grads[...] = block_layer(core[0, 0], got, w_first, w_second, mapped)
+        sums = chunk[:, :WIDTH]
+        d_users = chunk[:, WIDTH:]
+        z = jnp.dot(sums, w1, preferred_element_type=f32)
+        s = jax.nn.sigmoid(z)
+        hidden = (z * s).astype(bf16)
+        rows = slice(i * USERS, i * USERS + CHUNK)
+        sent[rows] = jnp.dot(hidden, w2, preferred_element_type=f32).astype(bf16)
+        back = lax.dot_general(d_users, w2, (((1,), (1,)), ((), ())), preferred_element_type=f32)
+        d_pre = (back * s * (1.0 + z * (1.0 - s))).astype(bf16)
+        grad_one += lax.dot_general(sums, d_pre, over_users, preferred_element_type=f32)
+        grad_two += lax.dot_general(hidden, d_users, over_users, preferred_element_type=f32)
+    is_first = core[0, 0] == 0
+    kept[...] = jnp.where(is_first, grad_one, grad_two)
+    sent[HALF:] = jnp.where(is_first, grad_two, grad_one).astype(bf16)
+
+
+def layer(core, got, w_first, w_second):
+    return pl.pallas_call(
+        layer_kernel,
+        out_shape=(
+            jax.ShapeDtypeStruct((HALF + WIDTH, WIDTH), bf16),
+            jax.ShapeDtypeStruct((WIDTH, WIDTH), f32),
+        ),
+        in_specs=[SMEM, VMEM, VMEM, VMEM],
+        out_specs=(VMEM, VMEM),
+        compiler_params=params(),
+        name="layer",
+    )(core, got, w_first, w_second)
+
+
+def own_kernel(sent, turned, out):
     for i in range(0, BLOCK, CHUNK):
-        out[i : i + CHUNK] = jnp.dot(turned[i : i + CHUNK, :HALF], mapped[...], preferred_element_type=f32)
-
-
-def own_product(core, got, w_first, w_second, turned):
+        out[i : i + CHUNK] = jnp.dot(turned[i : i + CHUNK, :HALF], sent[:HALF], preferred_element_type=f32)
+
+
+def own_product(sent, turned):
     return pl.pallas_call(
         own_kernel,
-        out_shape=(jax.ShapeDtypeStruct((BLOCK, WIDTH), f32), jax.ShapeDtypeStruct((WIDTH, WIDTH), f32)),
-        in_specs=[SMEM, VMEM, VMEM, VMEM, VMEM],
-        out_specs=(VMEM, VMEM),
-        scratch_shapes=[pltpu.VMEM((HALF, WIDTH), bf16)],
+        out_shape=jax.ShapeDtypeStruct((BLOCK, WIDTH), f32),
+        in_specs=[VMEM, VMEM],
+        out_specs=VMEM,
         compiler_params=params(),
         cost_estimate=cost(2 * BLOCK * HALF * WIDTH, 3 * 1024 * 1024),
         name="own_product",
-    )(core, got, w_first, w_second, turned)
-
-
-def back_kernel(core, got, w_first, w_second, own, own_grads, turned, out, mapped):
-    grads = own_grads[...] + block_layer(core[0, 0], got, w_first, w_second, mapped)
-    grads = grads.astype(bf16)
+    )(sent, turned)
+
+
+def back_kernel(got, own, kept, turned, out):
+    grads = (kept[...] + got[HALF:].astype(f32)).astype(bf16)
     for i in range(NEAR):
         rows = slice(i * CHUNK, (i + 1) * CHUNK)
-        part = own[rows] + jnp.dot(turned[rows, HALF:], mapped[...], preferred_element_type=f32)
+        part = own[rows] + jnp.dot(turned[rows, HALF:], got[:HALF], preferred_element_type=f32)
         out[i, :CHUNK] = part.astype(bf16)
         out[i, CHUNK:] = grads[SIDES[i] * ITEMS : (SIDES[i] + 1) * ITEMS]
 
 
-def back_product(core, got, w_first, w_second, own, own_grads, turned):
+def back_product(got, own, kept, turned):
     return pl.pallas_call(
         back_kernel,
         out_shape=jax.ShapeDtypeStruct((NEAR, CHUNK + ITEMS, WIDTH), bf16),
-        in_specs=[SMEM, VMEM, VMEM, VMEM, VMEM, VMEM, VMEM],
-        out_specs=VMEM,
-        scratch_shapes=[pltpu.VMEM((HALF, WIDTH), bf16)],
+        in_specs=[VMEM, VMEM, VMEM, VMEM],
+        out_specs=VMEM,
         compiler_params=params(),
         name="back_product",
-    )(core, got, w_first, w_second, own, own_grads, turned)
+    )(got, own, kept, turned)
 
 
 def sum_kernel(got, out):
@@ -321,7 +329,7 @@
     ]
     for half in range(2):
         for i in range(NEAR):
-            both[half, i * ITEMS : (i + 1) * ITEMS] = grads[half * NEAR + i].astype(f32)
+            both[half, SIDES[i] * ITEMS : (SIDES[i] + 1) * ITEMS] = grads[2 * i + half].astype(f32)
         copies[1 + half].start()
     total = got[0, :ITEMS].astype(f32)
     for i in range(1, NEAR):
@@ -355,7 +363,7 @@
     same_x = [[NEAR * i + k for k in range(NEAR)] for i in range(NEAR)]
     same_z = [[NEAR * i + k for i in SIDES] for k in range(NEAR)]
     sides = [
-        [(NEAR * i + k) * N_COL + 2 * q + h for h in range(2) for i in range(NEAR)]
+        [(NEAR * i + k) * N_COL + 2 * q + h for i in SIDES for h in range(2)]
         for k in range(NEAR)
         for q in range(PEERS)
     ]
@@ -372,9 +380,9 @@
     sums = half_product(add_kernel, bf16, mine, other, turned).reshape(PEERS, USERS, 2 * WIDTH)
     parts = lax.all_to_all(sums, "col", 0, 0, axis_index_groups=same_core)
     got = lax.all_to_all(middle(parts), "col", 0, 0, axis_index_groups=same_core)
-    other = lax.ppermute(got, "col", swap)
-    own, own_grads = own_product(core, got, w_first, w_second, turned)
-    sent = back_product(core, other, w_first, w_second, own, own_grads, turned)
+    mapped, kept = layer(core, got, w_first, w_second)
+    other = lax.ppermute(mapped, "col", swap)
+    sent = back_product(other, own_product(mapped, turned), kept, turned)
     sent = sum_sides(lax.all_to_all(sent, "row", 0, 0, axis_index_groups=same_z))
     got = lax.all_to_all(sent, "row", 0, 0, axis_index_groups=same_x)
     grads = lax.all_to_all(last_spread(got), ("row", "col"), 0, 0, axis_index_groups=sides)

time: 134 us -> 134 us (level)
  transfers between devices with their start and end apart: 3 -> 3, of which waited for: 3 -> 3; matrix products, arithmetic and copies ran while one was open for 0% -> 0% of each run, Pallas kernels for 4% -> 3%
where the time goes in v7:
time: 134 us; the launch traced here: 133 us
  blocking collectives  92.9 us (69%)
  starting transfers between devices  23.8 us (18%)
  Pallas kernels  8.66 us (6%)
  waiting for transfers between devices  6.26 us (5%)
  between operations  1.4 us (1%)
    all_to_all x1, blocking collectives, shards(): parts = lax.all_to_all(sums, 'col', 0, 0, axis_index_groups=same_core)  25.4 us
    all_to_all x1, blocking collectives, shards(): lax.all_to_all(middle(parts), 'col', 0, 0, axis_index_groups=same_core)  17.4 us
    all_to_all x1, blocking collectives, shards(): lax.all_to_all(second_spread(items, dense), 'row', 0, 0, axis_index_group...  14.2 us
    all_to_all x1, blocking collectives, shards(): lax.all_to_all(sent, 'row', 0, 0, axis_index_groups=same_z)  12.5 us
    all_to_all x1, blocking collectives, shards(): lax.all_to_all(last_spread(got), ('row', 'col'), 0, 0, axis_index_groups=...  12.5 us
    all_to_all x1, blocking collectives, shards(): got = lax.all_to_all(sent, 'row', 0, 0, axis_index_groups=same_x)  10.9 us
    all_to_all x1, starting transfers between devices, shards(): lax.all_to_all(spread, 'row', 0, 0, axis_index_groups=same_x)  10.9 us
    ppermute x1, starting transfers between devices, shards(): other = lax.ppermute(theirs, 'col', swap)  7.25 us
  transfers between devices with their start and end apart: 3, of which 3 were waited for; matrix products, arithmetic and copies ran while one was open for 0% of the time, Pallas kernels for 3%

profile of v7, /device:TPU:1, one launch (start us, length us, event | category | flops | bytes accessed | tf_op | source)
XLA Modules:
  0.0 133.0 jit_solution(5559544270157436214)
XLA Ops:
  0.6 1.5 %first_spread.1 = bf16[4,64,512]{2,1,0:T(8,128)(2,1)} custom-call(bf16[64,256]{1,0:T(8,128)(2,1)} %features.1, bf16[64,256]{1,0:T(8,128)(2,1)} %cotangent.1), custom_call_target="tpu_custom_call" | custom-call | bytes 524288 | tf_op jit(solution)/shard_map/first_spread/pallas_call | solution.py:59
  2.2 10.9 %all-to-all-start = ((bf16[4,64,512]{2,1,0:T(8,128)(2,1)}), bf16[4,64,512]{2,1,0:T(8,128)(2,1)S(1)}, u32[]{:S(2)}, u32[]{:S(2)}) async-start(bf16[4,64,512]{2,1,0:T(8,128)(2,1)} %first_spread.1), calls=%async_computation | async-start | bytes 524288 | tf_op jit(solution)/shard_map/all_to_all | solution.py:373
  13.7 2.2 %dense_block.1.after.dense = bf16[2,512,1024]{2,1,0:T(8,128)(2,1)S(1)} custom-call(s32[1,1]{1,0:T(1,128)} %bitcast.core, s32[1,1]{1,0:T(1,128)S(6)} %copy.10.count, s32[2,64]{1,0:T(2,128)} %bitcast.11, bf16[64,128,128]{2,1,0:T(8,128)(2,1)} %bitcast.10), custom_call_target="tpu_custom_call" | custom-call | bytes 6291456 | tf_op jit(solution)/shard_map/dense_block/pallas_call | solution.py:122
  15.9 5.3 %all-to-all-done = bf16[4,64,512]{2,1,0:T(8,128)(2,1)S(1)} async-done(((bf16[4,64,512]{2,1,0:T(8,128)(2,1)}), bf16[4,64,512]{2,1,0:T(8,128)(2,1)S(1)}, u32[]{:S(2)}, u32[]{:S(2)}) %all-to-all-start) | async-done | bytes 262176 | tf_op jit(solution)/shard_map/all_to_all | solution.py:373
  21.2 0.1 second_spread.1
  21.2 14.2 %all_to_all.35 = bf16[4,256,512]{2,1,0:T(8,128)(2,1)S(1)} all-to-all(bf16[4,256,512]{2,1,0:T(8,128)(2,1)S(1)} %second_spread.1), channel_id=1, replica_groups={{0,256,128,384},{32,288,160,416},{64,320,192,448},{96,352,224,480},{1,2..., dimensions={0} | all-to-all | bytes 2097152 | tf_op jit(solution)/shard_map/all_to_all | solution.py:374
  35.5 0.7 user_product.4.after
  36.2 7.3 %collective-permute-start = (bf16[512,512]{1,0:T(8,128)(2,1)S(1)}, bf16[512,512]{1,0:T(8,128)(2,1)S(1)}, u32[]{:S(2)}, u32[]{:S(2)}) collective-permute-start(bf16[512,512]{1,0:T(8,128)(2,1)S(1)} %user_product.4.after), channel_id=1, source_target_pairs={{0,1},{1,0},{2,3},{3,2},{4,5},{5,4},{6,7},{7,6},{8,9},{9,8},{10,11... | collective-permute-start | bytes 1572872 | tf_op jit(solution)/shard_map/ppermute | solution.py:377
  43.4 0.7 turned_block.1.after.turned
  44.1 0.7 user_product.3.mine
  44.8 0.1 collective-permute-done.other
  44.9 0.1 user_product.5
  45.0 0.0 copy-start
  45.0 0.0 copy-start.1
  45.1 25.4 %all_to_all.36.parts = bf16[16,32,512]{2,1,0:T(8,128)(2,1)S(1)} all-to-all(bf16[16,32,512]{2,1,0:T(8,128)(2,1)S(1)} %bitcast.8), channel_id=1, replica_groups={{0,28,4,24,8,20,12,16,2,30,6,26,10,22,14,18},{1,29,5,25,9,21,13,17,3,31..., dimensions={0} | all-to-all | bytes 1048576 | tf_op jit(solution)/shard_map/all_to_all | solution.py:381
  70.5 0.1 middle.1
  70.5 17.4 %all_to_all.37.got = bf16[16,32,512]{2,1,0:T(8,128)(2,1)S(1)} all-to-all(bf16[16,32,512]{2,1,0:T(8,128)(2,1)S(1)} %middle.1), channel_id=1, replica_groups={{0,28,4,24,8,20,12,16,2,30,6,26,10,22,14,18},{1,29,5,25,9,21,13,17,3,31..., dimensions={0} | all-to-all | bytes 1048576 | tf_op jit(solution)/shard_map/all_to_all | solution.py:382
  88.0 0.0 copy-done
  88.0 0.0 copy-done.1
  88.0 0.8 layer.1
  88.8 5.7 %collective-permute-start.1 = (bf16[768,256]{1,0:T(8,128)(2,1)S(1)}, bf16[768,256]{1,0:T(8,128)(2,1)S(1)}, u32[]{:S(2)}, u32[]{:S(2)}) collective-permute-start(bf16[768,256]{1,0:T(8,128)(2,1)S(1)} %get-tuple-element.5.sent), channel_id=1, source_target_pairs={{0,1},{1,0},{2,3},{3,2},{4,5},{5,4},{6,7},{7,6},{8,9},{9,8},{10,11... | collective-permute-start | bytes 1179656 | tf_op jit(solution)/shard_map/ppermute | solution.py:384
  94.5 0.4 own_product.1.own
  94.9 0.9 collective-permute-done.1.got
  95.8 0.5 back_product.1
  96.3 12.5 %all_to_all.38.got = bf16[4,320,256]{2,1,0:T(8,128)(2,1)S(1)} all-to-all(bf16[4,320,256]{2,1,0:T(8,128)(2,1)S(1)} %back_product.1), channel_id=1, replica_groups={{0,256,128,384},{32,288,160,416},{64,320,192,448},{96,352,224,480},{1,2..., dimensions={0} | all-to-all | bytes 1310720 | tf_op jit(solution)/shard_map/all_to_all | solution.py:386
  108.8 0.1 sum_sides.1
  108.8 10.9 %all_to_all.39.got = bf16[4,128,256]{2,1,0:T(8,128)(2,1)S(1)} all-to-all(bf16[4,128,256]{2,1,0:T(8,128)(2,1)S(1)} %sum_sides.1), channel_id=1, replica_groups={{0,32,64,96},{128,160,192,224},{256,288,320,352},{384,416,448,480},{1,3..., dimensions={0} | all-to-all | bytes 524288 | tf_op jit(solution)/shard_map/all_to_all | solution.py:387
  119.7 12.5 %all_to_all.40.grads = bf16[8,64,256]{2,1,0:T(8,128)(2,1)S(1)} all-to-all(bf16[8,64,256]{2,1,0:T(8,128)(2,1)S(1)} %last_spread.1), channel_id=1, replica_groups={{0,1,256,257,128,129,384,385},{2,3,258,259,130,131,386,387},{4,5,260,26..., dimensions={0} | all-to-all | bytes 524288 | tf_op jit(solution)/shard_map/all_to_all | solution.py:388
  132.2 0.8 finish.1
  (1 shorter events, 0.0 us)
Async XLA Ops:
  2.2 19.0 %all-to-all-start = ((bf16[4,64,512]{2,1,0:T(8,128)(2,1)}), bf16[4,64,512]{2,1,0:T(8,128)(2,1)S(1)}, u32[]{:S(2)}, u32[]{:S(2)}) async-start(bf16[4,64,512]{2,1,0:T(8,128)(2,1)} %first_spread.1), calls=%async_computation | async-start | bytes 524288 | tf_op jit(solution)/shard_map/all_to_all | solution.py:373
  36.2 8.8 %collective-permute-start = (bf16[512,512]{1,0:T(8,128)(2,1)S(1)}, bf16[512,512]{1,0:T(8,128)(2,1)S(1)}, u32[]{:S(2)}, u32[]{:S(2)}) collective-permute-start(bf16[512,512]{1,0:T(8,128)(2,1)S(1)} %user_product.4.after), channel_id=1, source_target_pairs={{0,1},{1,0},{2,3},{3,2},{4,5},{5,4},{6,7},{7,6},{8,9},{9,8},{10,11... | collective-permute-start | bytes 1572872 | tf_op jit(solution)/shard_map/ppermute | solution.py:377
  45.0 42.9 %copy-start = (bf16[256,256]{1,0:T(8,128)(2,1)S(1)}, bf16[256,256]{1,0:T(8,128)(2,1)}, u32[]{:S(2)}) copy-start(bf16[256,256]{1,0:T(8,128)(2,1)} %w_first.1) | copy-start | bytes 393220
  45.0 42.9 %copy-start.1 = (bf16[256,256]{1,0:T(8,128)(2,1)S(1)}, bf16[256,256]{1,0:T(8,128)(2,1)}, u32[]{:S(2)}) copy-start(bf16[256,256]{1,0:T(8,128)(2,1)} %w_second.1) | copy-start | bytes 393220
  88.8 7.0 %collective-permute-start.1 = (bf16[768,256]{1,0:T(8,128)(2,1)S(1)}, bf16[768,256]{1,0:T(8,128)(2,1)S(1)}, u32[]{:S(2)}, u32[]{:S(2)}) collective-permute-start(bf16[768,256]{1,0:T(8,128)(2,1)S(1)} %get-tuple-element.5.sent), channel_id=1, source_target_pairs={{0,1},{1,0},{2,3},{3,2},{4,5},{5,4},{6,7},{7,6},{8,9},{9,8},{10,11... | collective-permute-start | bytes 1179656 | tf_op jit(solution)/shard_map/ppermute | solution.py:384
